TPU v7x, 1024 devices: a whole 4x8x16 slice. The times are simulated.
1024 devices in a mesh: ax: 256 (over z, x, y_lo), rad: 4 (over y_hi, core).
Axes of the slice: x: 4, y: 8 (y_hi: 2, y_lo: 4; y = y_hi * 4 + y_lo), z: 16, core: 2. Of those that a mesh axis runs over, the one named last changes fastest.
Arguments:
- forcing_state: bfloat16 [512, 64, 16, 320], P('ax', 'rad'), may hold values from -6 to 6
- link_bits: int32 [512, 64, 4], P('ax', 'rad'), may hold values from 0 to 1, as said below
- couplings: bfloat16 [5, 320, 320], replicated, may hold values from -0.15625 to 0.15625
- shape_vectors: bfloat16 [512, 64, 320], P('ax', 'rad'), may hold values from -0.3125 to 0.3125
- actuator_map: int32 [512, 64], P('ax', 'rad'), may hold values from 0 to 4095, as said below
Outputs:
- adjoint_state: bfloat16 [512, 64, 16, 320], P('ax', 'rad')
- actuator_grad: float32 [16, 4096], P(None, ('ax', 'rad'))
Inputs may be any that keep to these rules, and one draw needn't show every extreme that they name: The pattern is symmetric: link_bits[i, j, 1] equals link_bits[i + 1, j, 0] and link_bits[i, j, 3] equals link_bits[i, j + 1, 2]. `actuator_map`: actuator a lies in the group a // 4; the group of block (i, j)'s actuator is (i // 2 + d) * 4 + j // 16 with d one of -1, 0, 1.
All inputs are finite; a program needn't handle non-finite values.
Results may differ from a plain program's by a relative error of at most 0.0065.
Values may be sent and summed in bfloat16 or wider, within the bound.
No kernel may reach another device: no remote copies, remote signals or barrier semaphores. Data moves between devices by JAX's collectives and lax.ppermute only.
A program may use at most 32 MiB of HBM per device.

v0:
```python
import jax
import jax.numpy as jnp
from jax import lax
from jax.sharding import PartitionSpec as P

ACT = 4096
STEPS = 2


def with_halo(block, sides, width):
    for axis, dim in sides:
        count = lax.axis_size(axis)
        forward = [(i, i + 1) for i in range(count - 1)]
        backward = [(target, source) for source, target in forward]
        low = lax.ppermute(
            lax.slice_in_dim(block, block.shape[dim] - width, None, axis=dim), axis, forward
        )
        high = lax.ppermute(lax.slice_in_dim(block, 0, width, axis=dim), axis, backward)
        block = jnp.concatenate([low, block, high], axis=dim)
    return block


def passed_along(x, axis, by):
    length = lax.axis_size(axis)
    pairs = [(i, i + by) for i in range(length) if 0 <= i + by < length]
    return lax.ppermute(x, axis, pairs)


def couple(field_now, matrix, adjoint):
    if adjoint:
        dims = (((3,), (1,)), ((), ()))
    else:
        dims = (((3,), (0,)), ((), ()))
    return lax.dot_general(field_now, matrix, dims, preferred_element_type=jnp.float32)


def advance(field_now, masks, couplings, adjoint):
    opposite = [1, 0, 3, 2]
    padded = with_halo(field_now, (("ax", 0), ("rad", 1)), 1)
    beside = [padded[:-2, 1:-1], padded[2:, 1:-1], padded[1:-1, :-2], padded[1:-1, 2:]]
    summed = couple(field_now, couplings[0], adjoint)
    for direction in range(4):
        if adjoint:
            matrix = couplings[opposite[direction] + 1]
        else:
            matrix = couplings[direction + 1]
        summed = summed + masks[:, :, direction][:, :, None, None] * couple(
            beside[direction], matrix, adjoint
        )
    return summed.astype(jnp.bfloat16)


def body(forcing_state, link_bits, couplings, shape_vectors, actuator_map):
    masks = link_bits.astype(jnp.float32)
    field_now = forcing_state
    for repeat in range(STEPS):
        field_now = advance(field_now, masks, couplings, False)
    for repeat in range(STEPS):
        field_now = advance(field_now, masks, couplings, True)
    projected = jnp.einsum(
        "xyfk,xyk->xyf", field_now, shape_vectors, preferred_element_type=jnp.float32
    )
    forcings = projected.shape[-1]
    projected = projected.reshape(-1, forcings)
    count_ax = lax.axis_size("ax")
    count_rad = lax.axis_size("rad")
    per_group = ACT // (count_ax * count_rad)
    my_group = lax.axis_index("ax") * count_rad + lax.axis_index("rad")
    flat_map = actuator_map.reshape(-1)
    group_of = flat_map // per_group
    column = ((group_of - my_group) // count_rad + 1) * per_group + flat_map % per_group
    one_hot = (column[:, None] == jnp.arange(3 * per_group, dtype=jnp.int32)[None, :]).astype(
        jnp.float32
    )
    partial_grad = lax.dot_general(
        projected,
        one_hot,
        (((0,), (0,)), ((), ())),
        precision=lax.Precision.HIGHEST,
        preferred_element_type=jnp.float32,
    )
    to_prev = partial_grad[:, :per_group]
    own_part = partial_grad[:, per_group : 2 * per_group]
    to_next = partial_grad[:, 2 * per_group :]
    from_prev = passed_along(to_next, "ax", 1)
    from_next = passed_along(to_prev, "ax", -1)
    grad_share = own_part + from_prev + from_next
    return (field_now, grad_share)


def solution(mesh):
    in_specs = (
        P("ax", "rad", None, None),
        P("ax", "rad", None),
        P(),
        P("ax", "rad", None),
        P("ax", "rad"),
    )
    out_specs = (P("ax", "rad", None, None), P(None, ("ax", "rad")))
    return jax.shard_map(body, mesh=mesh, in_specs=in_specs, out_specs=out_specs, check_vma=False)
```

profile of v0, /device:TPU:479, one launch (start us, length us, event | category | flops | bytes accessed | tf_op | source)
XLA Modules:
  0.0 144.5 jit_solution(17544634996220394180)
XLA Ops:
  1.8 4.8 %collective-permute-start = (bf16[1,16,16,320]{3,2,1,0:T(8,128)(2,1)S(1)}, bf16[1,16,16,320]{3,2,1,0:T(8,128)(2,1)S(1)}, u32[]{:S(2)}, u32[]{:S(2)}) collective-permute-start(bf16[1,16,16,320]{3,2,1,0:T(8,128)(2,1)S(1)} %get-tuple-element.17), channel_id=1, source_target_pairs={{0,4},{4,8},{8,12},{12,16},{16,20},{20,24},{24,28},{28,32},{32,36}... | collective-permute-start | bytes 491528 | tf_op jit(solution)/shard_map/ppermute | solution.py:15
  6.6 1.9 %collective-permute-start.1 = (bf16[1,16,16,320]{3,2,1,0:T(8,128)(2,1)S(1)}, bf16[1,16,16,320]{3,2,1,0:T(8,128)(2,1)S(1)}, u32[]{:S(2)}, u32[]{:S(2)}) collective-permute-start(bf16[1,16,16,320]{3,2,1,0:T(8,128)(2,1)S(1)} %get-tuple-element.16), channel_id=1, source_target_pairs={{4,0},{8,4},{12,8},{16,12},{20,16},{24,20},{28,24},{32,28},{36,32}... | collective-permute-start | bytes 491528 | tf_op jit(solution)/shard_map/ppermute | solution.py:18
  10.9 9.0 %collective-permute-done.1 = bf16[1,16,16,320]{3,2,1,0:T(8,128)(2,1)S(1)} collective-permute-done((bf16[1,16,16,320]{3,2,1,0:T(8,128)(2,1)S(1)}, bf16[1,16,16,320]{3,2,1,0:T(8,128)(2,1)S(1)}, u32[]{:S(2)}, u32[]{:S(2)}) %collective-permute-start.1) | collective-permute-done | bytes 163872 | tf_op jit(solution)/shard_map/ppermute | solution.py:18
  20.0 9.2 %collective-permute-start.2 = (bf16[4,1,16,320]{3,2,1,0:T(8,128)(2,1)S(1)}, bf16[4,1,16,320]{3,2,1,0:T(8,128)(2,1)S(1)}, u32[]{:S(2)}, u32[]{:S(2)}) collective-permute-start(bf16[4,1,16,320]{3,2,1,0:T(8,128)(2,1)S(1)} %get-tuple-element.8), channel_id=1, source_target_pairs={{0,1},{1,2},{2,3},{4,5},{5,6},{6,7},{8,9},{9,10},{10,11},{12,13},{... | collective-permute-start | bytes 122888 | tf_op jit(solution)/shard_map/ppermute | solution.py:15
  29.2 1.9 %collective-permute-start.3 = (bf16[4,1,16,320]{3,2,1,0:T(8,128)(2,1)S(1)}, bf16[4,1,16,320]{3,2,1,0:T(8,128)(2,1)S(1)}, u32[]{:S(2)}, u32[]{:S(2)}) collective-permute-start(bf16[4,1,16,320]{3,2,1,0:T(8,128)(2,1)S(1)} %get-tuple-element.9), channel_id=1, source_target_pairs={{1,0},{2,1},{3,2},{5,4},{6,5},{7,6},{9,8},{10,9},{11,10},{13,12},{... | collective-permute-start | bytes 122888 | tf_op jit(solution)/shard_map/ppermute | solution.py:18
  31.9 6.7 %collective-permute-done.3 = bf16[4,1,16,320]{3,2,1,0:T(8,128)(2,1)S(1)} collective-permute-done((bf16[4,1,16,320]{3,2,1,0:T(8,128)(2,1)S(1)}, bf16[4,1,16,320]{3,2,1,0:T(8,128)(2,1)S(1)}, u32[]{:S(2)}, u32[]{:S(2)}) %collective-permute-start.3) | collective-permute-done | bytes 40992 | tf_op jit(solution)/shard_map/ppermute | solution.py:18
  39.6 1.9 %collective-permute-start.5 = (bf16[1,16,16,320]{3,2,1,0:T(8,128)(2,1)S(1)}, bf16[1,16,16,320]{3,2,1,0:T(8,128)(2,1)S(1)}, u32[]{:S(2)}, u32[]{:S(2)}) collective-permute-start(bf16[1,16,16,320]{3,2,1,0:T(8,128)(2,1)S(1)} %get-tuple-element.15), channel_id=1, source_target_pairs={{4,0},{8,4},{12,8},{16,12},{20,16},{24,20},{28,24},{32,28},{36,32}... | collective-permute-start | bytes 491528 | tf_op jit(solution)/shard_map/ppermute | solution.py:18
  41.5 9.4 %collective-permute-start.4 = (bf16[1,16,16,320]{3,2,1,0:T(8,128)(2,1)S(1)}, bf16[1,16,16,320]{3,2,1,0:T(8,128)(2,1)S(1)}, u32[]{:S(2)}, u32[]{:S(2)}) collective-permute-start(bf16[1,16,16,320]{3,2,1,0:T(8,128)(2,1)S(1)} %get-tuple-element.14), channel_id=1, source_target_pairs={{0,4},{4,8},{8,12},{12,16},{16,20},{20,24},{24,28},{28,32},{32,36}... | collective-permute-start | bytes 491528 | tf_op jit(solution)/shard_map/ppermute | solution.py:15
  53.6 2.9 %collective-permute-start.6 = (bf16[4,1,16,320]{3,2,1,0:T(8,128)(2,1)S(1)}, bf16[4,1,16,320]{3,2,1,0:T(8,128)(2,1)S(1)}, u32[]{:S(2)}, u32[]{:S(2)}) collective-permute-start(bf16[4,1,16,320]{3,2,1,0:T(8,128)(2,1)S(1)} %get-tuple-element.6), channel_id=1, source_target_pairs={{0,1},{1,2},{2,3},{4,5},{5,6},{6,7},{8,9},{9,10},{10,11},{12,13},{... | collective-permute-start | bytes 122888 | tf_op jit(solution)/shard_map/ppermute | solution.py:15
  56.4 1.9 %collective-permute-start.7 = (bf16[4,1,16,320]{3,2,1,0:T(8,128)(2,1)S(1)}, bf16[4,1,16,320]{3,2,1,0:T(8,128)(2,1)S(1)}, u32[]{:S(2)}, u32[]{:S(2)}) collective-permute-start(bf16[4,1,16,320]{3,2,1,0:T(8,128)(2,1)S(1)} %get-tuple-element.7), channel_id=1, source_target_pairs={{1,0},{2,1},{3,2},{5,4},{6,5},{7,6},{9,8},{10,9},{11,10},{13,12},{... | collective-permute-start | bytes 122888 | tf_op jit(solution)/shard_map/ppermute | solution.py:18
  59.1 6.8 %collective-permute-done.7 = bf16[4,1,16,320]{3,2,1,0:T(8,128)(2,1)S(1)} collective-permute-done((bf16[4,1,16,320]{3,2,1,0:T(8,128)(2,1)S(1)}, bf16[4,1,16,320]{3,2,1,0:T(8,128)(2,1)S(1)}, u32[]{:S(2)}, u32[]{:S(2)}) %collective-permute-start.7) | collective-permute-done | bytes 40992 | tf_op jit(solution)/shard_map/ppermute | solution.py:18
  66.9 1.9 %collective-permute-start.9 = (bf16[1,16,16,320]{3,2,1,0:T(8,128)(2,1)S(1)}, bf16[1,16,16,320]{3,2,1,0:T(8,128)(2,1)S(1)}, u32[]{:S(2)}, u32[]{:S(2)}) collective-permute-start(bf16[1,16,16,320]{3,2,1,0:T(8,128)(2,1)S(1)} %get-tuple-element.13), channel_id=1, source_target_pairs={{4,0},{8,4},{12,8},{16,12},{20,16},{24,20},{28,24},{32,28},{36,32}... | collective-permute-start | bytes 491528 | tf_op jit(solution)/shard_map/ppermute | solution.py:18
  68.8 10.6 %collective-permute-start.8 = (bf16[1,16,16,320]{3,2,1,0:T(8,128)(2,1)S(1)}, bf16[1,16,16,320]{3,2,1,0:T(8,128)(2,1)S(1)}, u32[]{:S(2)}, u32[]{:S(2)}) collective-permute-start(bf16[1,16,16,320]{3,2,1,0:T(8,128)(2,1)S(1)} %get-tuple-element.12), channel_id=1, source_target_pairs={{0,4},{4,8},{8,12},{12,16},{16,20},{20,24},{24,28},{28,32},{32,36}... | collective-permute-start | bytes 491528 | tf_op jit(solution)/shard_map/ppermute | solution.py:15
  82.1 2.6 %collective-permute-start.10 = (bf16[4,1,16,320]{3,2,1,0:T(8,128)(2,1)S(1)}, bf16[4,1,16,320]{3,2,1,0:T(8,128)(2,1)S(1)}, u32[]{:S(2)}, u32[]{:S(2)}) collective-permute-start(bf16[4,1,16,320]{3,2,1,0:T(8,128)(2,1)S(1)} %get-tuple-element.4), channel_id=1, source_target_pairs={{0,1},{1,2},{2,3},{4,5},{5,6},{6,7},{8,9},{9,10},{10,11},{12,13},{... | collective-permute-start | bytes 122888 | tf_op jit(solution)/shard_map/ppermute | solution.py:15
  84.7 1.9 %collective-permute-start.11 = (bf16[4,1,16,320]{3,2,1,0:T(8,128)(2,1)S(1)}, bf16[4,1,16,320]{3,2,1,0:T(8,128)(2,1)S(1)}, u32[]{:S(2)}, u32[]{:S(2)}) collective-permute-start(bf16[4,1,16,320]{3,2,1,0:T(8,128)(2,1)S(1)} %get-tuple-element.5), channel_id=1, source_target_pairs={{1,0},{2,1},{3,2},{5,4},{6,5},{7,6},{9,8},{10,9},{11,10},{13,12},{... | collective-permute-start | bytes 122888 | tf_op jit(solution)/shard_map/ppermute | solution.py:18
  87.5 6.6 %collective-permute-done.11 = bf16[4,1,16,320]{3,2,1,0:T(8,128)(2,1)S(1)} collective-permute-done((bf16[4,1,16,320]{3,2,1,0:T(8,128)(2,1)S(1)}, bf16[4,1,16,320]{3,2,1,0:T(8,128)(2,1)S(1)}, u32[]{:S(2)}, u32[]{:S(2)}) %collective-permute-start.11) | collective-permute-done | bytes 40992 | tf_op jit(solution)/shard_map/ppermute | solution.py:18
  95.1 1.9 %collective-permute-start.13 = (bf16[1,16,16,320]{3,2,1,0:T(8,128)(2,1)S(1)}, bf16[1,16,16,320]{3,2,1,0:T(8,128)(2,1)S(1)}, u32[]{:S(2)}, u32[]{:S(2)}) collective-permute-start(bf16[1,16,16,320]{3,2,1,0:T(8,128)(2,1)S(1)} %get-tuple-element.11), channel_id=1, source_target_pairs={{4,0},{8,4},{12,8},{16,12},{20,16},{24,20},{28,24},{32,28},{36,32}... | collective-permute-start | bytes 491528 | tf_op jit(solution)/shard_map/ppermute | solution.py:18
  97.0 10.3 %collective-permute-start.12 = (bf16[1,16,16,320]{3,2,1,0:T(8,128)(2,1)S(1)}, bf16[1,16,16,320]{3,2,1,0:T(8,128)(2,1)S(1)}, u32[]{:S(2)}, u32[]{:S(2)}) collective-permute-start(bf16[1,16,16,320]{3,2,1,0:T(8,128)(2,1)S(1)} %get-tuple-element.10), channel_id=1, source_target_pairs={{0,4},{4,8},{8,12},{12,16},{16,20},{20,24},{24,28},{28,32},{32,36}... | collective-permute-start | bytes 491528 | tf_op jit(solution)/shard_map/ppermute | solution.py:15
  109.9 2.7 %collective-permute-start.14 = (bf16[4,1,16,320]{3,2,1,0:T(8,128)(2,1)S(1)}, bf16[4,1,16,320]{3,2,1,0:T(8,128)(2,1)S(1)}, u32[]{:S(2)}, u32[]{:S(2)}) collective-permute-start(bf16[4,1,16,320]{3,2,1,0:T(8,128)(2,1)S(1)} %get-tuple-element.2), channel_id=1, source_target_pairs={{0,1},{1,2},{2,3},{4,5},{5,6},{6,7},{8,9},{9,10},{10,11},{12,13},{... | collective-permute-start | bytes 122888 | tf_op jit(solution)/shard_map/ppermute | solution.py:15
  112.6 1.9 %collective-permute-start.15 = (bf16[4,1,16,320]{3,2,1,0:T(8,128)(2,1)S(1)}, bf16[4,1,16,320]{3,2,1,0:T(8,128)(2,1)S(1)}, u32[]{:S(2)}, u32[]{:S(2)}) collective-permute-start(bf16[4,1,16,320]{3,2,1,0:T(8,128)(2,1)S(1)} %get-tuple-element.3), channel_id=1, source_target_pairs={{1,0},{2,1},{3,2},{5,4},{6,5},{7,6},{9,8},{10,9},{11,10},{13,12},{... | collective-permute-start | bytes 122888 | tf_op jit(solution)/shard_map/ppermute | solution.py:18
  115.4 6.5 %collective-permute-done.15 = bf16[4,1,16,320]{3,2,1,0:T(8,128)(2,1)S(1)} collective-permute-done((bf16[4,1,16,320]{3,2,1,0:T(8,128)(2,1)S(1)}, bf16[4,1,16,320]{3,2,1,0:T(8,128)(2,1)S(1)}, u32[]{:S(2)}, u32[]{:S(2)}) %collective-permute-start.15) | collective-permute-done | bytes 40992 | tf_op jit(solution)/shard_map/ppermute | solution.py:18
  123.4 10.2 %collective-permute-start.16 = (f32[16,4]{0,1:T(4,128)S(1)}, f32[16,4]{0,1:T(4,128)S(1)}, u32[]{:S(2)}, u32[]{:S(2)}) collective-permute-start(f32[16,4]{0,1:T(4,128)S(1)} %get-tuple-element.18), channel_id=1, source_target_pairs={{0,4},{4,8},{8,12},{12,16},{16,20},{20,24},{24,28},{28,32},{32,36}... | collective-permute-start | bytes 776 | tf_op jit(solution)/shard_map/ppermute | solution.py:26
  133.6 1.9 %collective-permute-start.17 = (f32[16,4]{0,1:T(4,128)S(1)}, f32[16,4]{0,1:T(4,128)S(1)}, u32[]{:S(2)}, u32[]{:S(2)}) collective-permute-start(f32[16,4]{0,1:T(4,128)S(1)} %get-tuple-element.19), channel_id=1, source_target_pairs={{4,0},{8,4},{12,8},{16,12},{20,16},{24,20},{28,24},{32,28},{36,32}... | collective-permute-start | bytes 776 | tf_op jit(solution)/shard_map/ppermute | solution.py:26
  135.5 8.4 %collective-permute-done.17 = f32[16,4]{0,1:T(4,128)S(1)} collective-permute-done((f32[16,4]{0,1:T(4,128)S(1)}, f32[16,4]{0,1:T(4,128)S(1)}, u32[]{:S(2)}, u32[]{:S(2)}) %collective-permute-start.17) | collective-permute-done | bytes 288 | tf_op jit(solution)/shard_map/ppermute | solution.py:26
  (61 shorter events, 19.3 us)
Async XLA Ops:
  0.6 122.2 %copy-start = (bf16[2,16,320]{2,1,0:T(8,128)(2,1)S(1)}, bf16[2,16,320]{2,1,0:T(8,128)(2,1)}, u32[]{:S(2)}) copy-start(bf16[2,16,320]{2,1,0:T(8,128)(2,1)} %param.8) | copy-start | bytes 61444
  0.6 10.2 %copy-start.1 = (bf16[2,16,16,320]{3,2,1,0:T(8,128)(2,1)S(1)}, bf16[2,16,16,320]{3,2,1,0:T(8,128)(2,1)}, u32[]{:S(2)}) copy-start(bf16[2,16,16,320]{3,2,1,0:T(8,128)(2,1)} %param.5) | copy-start | bytes 983044
  0.7 10.0 %copy-start.4 = (s32[2,16]{1,0:T(2,128)S(1)}, s32[2,16]{1,0:T(2,128)}, u32[]{:S(2)}) copy-start(s32[2,16]{1,0:T(2,128)} %param.9) | copy-start | bytes 388
  1.8 9.0 %collective-permute-start = (bf16[1,16,16,320]{3,2,1,0:T(8,128)(2,1)S(1)}, bf16[1,16,16,320]{3,2,1,0:T(8,128)(2,1)S(1)}, u32[]{:S(2)}, u32[]{:S(2)}) collective-permute-start(bf16[1,16,16,320]{3,2,1,0:T(8,128)(2,1)S(1)} %get-tuple-element.17), channel_id=1, source_target_pairs={{0,4},{4,8},{8,12},{12,16},{16,20},{20,24},{24,28},{28,32},{32,36}... | collective-permute-start | bytes 491528 | tf_op jit(solution)/shard_map/ppermute | solution.py:15
  6.6 13.4 %collective-permute-start.1 = (bf16[1,16,16,320]{3,2,1,0:T(8,128)(2,1)S(1)}, bf16[1,16,16,320]{3,2,1,0:T(8,128)(2,1)S(1)}, u32[]{:S(2)}, u32[]{:S(2)}) collective-permute-start(bf16[1,16,16,320]{3,2,1,0:T(8,128)(2,1)S(1)} %get-tuple-element.16), channel_id=1, source_target_pairs={{4,0},{8,4},{12,8},{16,12},{20,16},{24,20},{28,24},{32,28},{36,32}... | collective-permute-start | bytes 491528 | tf_op jit(solution)/shard_map/ppermute | solution.py:18
  10.7 20.5 %copy-start.2 = (bf16[5,320,320]{2,1,0:T(8,128)(2,1)S(1)}, bf16[5,320,320]{2,1,0:T(8,128)(2,1)}, u32[]{:S(2)}) copy-start(bf16[5,320,320]{2,1,0:T(8,128)(2,1)} %param.7) | copy-start | bytes 3072004
  20.0 11.5 %collective-permute-start.2 = (bf16[4,1,16,320]{3,2,1,0:T(8,128)(2,1)S(1)}, bf16[4,1,16,320]{3,2,1,0:T(8,128)(2,1)S(1)}, u32[]{:S(2)}, u32[]{:S(2)}) collective-permute-start(bf16[4,1,16,320]{3,2,1,0:T(8,128)(2,1)S(1)} %get-tuple-element.8), channel_id=1, source_target_pairs={{0,1},{1,2},{2,3},{4,5},{5,6},{6,7},{8,9},{9,10},{10,11},{12,13},{... | collective-permute-start | bytes 122888 | tf_op jit(solution)/shard_map/ppermute | solution.py:15
  29.2 9.5 %collective-permute-start.3 = (bf16[4,1,16,320]{3,2,1,0:T(8,128)(2,1)S(1)}, bf16[4,1,16,320]{3,2,1,0:T(8,128)(2,1)S(1)}, u32[]{:S(2)}, u32[]{:S(2)}) collective-permute-start(bf16[4,1,16,320]{3,2,1,0:T(8,128)(2,1)S(1)} %get-tuple-element.9), channel_id=1, source_target_pairs={{1,0},{2,1},{3,2},{5,4},{6,5},{7,6},{9,8},{10,9},{11,10},{13,12},{... | collective-permute-start | bytes 122888 | tf_op jit(solution)/shard_map/ppermute | solution.py:18
  39.6 12.5 %collective-permute-start.5 = (bf16[1,16,16,320]{3,2,1,0:T(8,128)(2,1)S(1)}, bf16[1,16,16,320]{3,2,1,0:T(8,128)(2,1)S(1)}, u32[]{:S(2)}, u32[]{:S(2)}) collective-permute-start(bf16[1,16,16,320]{3,2,1,0:T(8,128)(2,1)S(1)} %get-tuple-element.15), channel_id=1, source_target_pairs={{4,0},{8,4},{12,8},{16,12},{20,16},{24,20},{28,24},{32,28},{36,32}... | collective-permute-start | bytes 491528 | tf_op jit(solution)/shard_map/ppermute | solution.py:18
  41.5 12.0 %collective-permute-start.4 = (bf16[1,16,16,320]{3,2,1,0:T(8,128)(2,1)S(1)}, bf16[1,16,16,320]{3,2,1,0:T(8,128)(2,1)S(1)}, u32[]{:S(2)}, u32[]{:S(2)}) collective-permute-start(bf16[1,16,16,320]{3,2,1,0:T(8,128)(2,1)S(1)} %get-tuple-element.14), channel_id=1, source_target_pairs={{0,4},{4,8},{8,12},{12,16},{16,20},{20,24},{24,28},{28,32},{32,36}... | collective-permute-start | bytes 491528 | tf_op jit(solution)/shard_map/ppermute | solution.py:15
  53.6 5.2 %collective-permute-start.6 = (bf16[4,1,16,320]{3,2,1,0:T(8,128)(2,1)S(1)}, bf16[4,1,16,320]{3,2,1,0:T(8,128)(2,1)S(1)}, u32[]{:S(2)}, u32[]{:S(2)}) collective-permute-start(bf16[4,1,16,320]{3,2,1,0:T(8,128)(2,1)S(1)} %get-tuple-element.6), channel_id=1, source_target_pairs={{0,1},{1,2},{2,3},{4,5},{5,6},{6,7},{8,9},{9,10},{10,11},{12,13},{... | collective-permute-start | bytes 122888 | tf_op jit(solution)/shard_map/ppermute | solution.py:15
  56.4 9.5 %collective-permute-start.7 = (bf16[4,1,16,320]{3,2,1,0:T(8,128)(2,1)S(1)}, bf16[4,1,16,320]{3,2,1,0:T(8,128)(2,1)S(1)}, u32[]{:S(2)}, u32[]{:S(2)}) collective-permute-start(bf16[4,1,16,320]{3,2,1,0:T(8,128)(2,1)S(1)} %get-tuple-element.7), channel_id=1, source_target_pairs={{1,0},{2,1},{3,2},{5,4},{6,5},{7,6},{9,8},{10,9},{11,10},{13,12},{... | collective-permute-start | bytes 122888 | tf_op jit(solution)/shard_map/ppermute | solution.py:18
  66.9 13.8 %collective-permute-start.9 = (bf16[1,16,16,320]{3,2,1,0:T(8,128)(2,1)S(1)}, bf16[1,16,16,320]{3,2,1,0:T(8,128)(2,1)S(1)}, u32[]{:S(2)}, u32[]{:S(2)}) collective-permute-start(bf16[1,16,16,320]{3,2,1,0:T(8,128)(2,1)S(1)} %get-tuple-element.13), channel_id=1, source_target_pairs={{4,0},{8,4},{12,8},{16,12},{20,16},{24,20},{28,24},{32,28},{36,32}... | collective-permute-start | bytes 491528 | tf_op jit(solution)/shard_map/ppermute | solution.py:18
  68.8 13.2 %collective-permute-start.8 = (bf16[1,16,16,320]{3,2,1,0:T(8,128)(2,1)S(1)}, bf16[1,16,16,320]{3,2,1,0:T(8,128)(2,1)S(1)}, u32[]{:S(2)}, u32[]{:S(2)}) collective-permute-start(bf16[1,16,16,320]{3,2,1,0:T(8,128)(2,1)S(1)} %get-tuple-element.12), channel_id=1, source_target_pairs={{0,4},{4,8},{8,12},{12,16},{16,20},{20,24},{24,28},{28,32},{32,36}... | collective-permute-start | bytes 491528 | tf_op jit(solution)/shard_map/ppermute | solution.py:15
  82.1 5.0 %collective-permute-start.10 = (bf16[4,1,16,320]{3,2,1,0:T(8,128)(2,1)S(1)}, bf16[4,1,16,320]{3,2,1,0:T(8,128)(2,1)S(1)}, u32[]{:S(2)}, u32[]{:S(2)}) collective-permute-start(bf16[4,1,16,320]{3,2,1,0:T(8,128)(2,1)S(1)} %get-tuple-element.4), channel_id=1, source_target_pairs={{0,1},{1,2},{2,3},{4,5},{5,6},{6,7},{8,9},{9,10},{10,11},{12,13},{... | collective-permute-start | bytes 122888 | tf_op jit(solution)/shard_map/ppermute | solution.py:15
  84.7 9.4 %collective-permute-start.11 = (bf16[4,1,16,320]{3,2,1,0:T(8,128)(2,1)S(1)}, bf16[4,1,16,320]{3,2,1,0:T(8,128)(2,1)S(1)}, u32[]{:S(2)}, u32[]{:S(2)}) collective-permute-start(bf16[4,1,16,320]{3,2,1,0:T(8,128)(2,1)S(1)} %get-tuple-element.5), channel_id=1, source_target_pairs={{1,0},{2,1},{3,2},{5,4},{6,5},{7,6},{9,8},{10,9},{11,10},{13,12},{... | collective-permute-start | bytes 122888 | tf_op jit(solution)/shard_map/ppermute | solution.py:18
  95.1 13.4 %collective-permute-start.13 = (bf16[1,16,16,320]{3,2,1,0:T(8,128)(2,1)S(1)}, bf16[1,16,16,320]{3,2,1,0:T(8,128)(2,1)S(1)}, u32[]{:S(2)}, u32[]{:S(2)}) collective-permute-start(bf16[1,16,16,320]{3,2,1,0:T(8,128)(2,1)S(1)} %get-tuple-element.11), channel_id=1, source_target_pairs={{4,0},{8,4},{12,8},{16,12},{20,16},{24,20},{28,24},{32,28},{36,32}... | collective-permute-start | bytes 491528 | tf_op jit(solution)/shard_map/ppermute | solution.py:18
  97.0 12.9 %collective-permute-start.12 = (bf16[1,16,16,320]{3,2,1,0:T(8,128)(2,1)S(1)}, bf16[1,16,16,320]{3,2,1,0:T(8,128)(2,1)S(1)}, u32[]{:S(2)}, u32[]{:S(2)}) collective-permute-start(bf16[1,16,16,320]{3,2,1,0:T(8,128)(2,1)S(1)} %get-tuple-element.10), channel_id=1, source_target_pairs={{0,4},{4,8},{8,12},{12,16},{16,20},{20,24},{24,28},{28,32},{32,36}... | collective-permute-start | bytes 491528 | tf_op jit(solution)/shard_map/ppermute | solution.py:15
  109.9 5.1 %collective-permute-start.14 = (bf16[4,1,16,320]{3,2,1,0:T(8,128)(2,1)S(1)}, bf16[4,1,16,320]{3,2,1,0:T(8,128)(2,1)S(1)}, u32[]{:S(2)}, u32[]{:S(2)}) collective-permute-start(bf16[4,1,16,320]{3,2,1,0:T(8,128)(2,1)S(1)} %get-tuple-element.2), channel_id=1, source_target_pairs={{0,1},{1,2},{2,3},{4,5},{5,6},{6,7},{8,9},{9,10},{10,11},{12,13},{... | collective-permute-start | bytes 122888 | tf_op jit(solution)/shard_map/ppermute | solution.py:15
  112.6 9.3 %collective-permute-start.15 = (bf16[4,1,16,320]{3,2,1,0:T(8,128)(2,1)S(1)}, bf16[4,1,16,320]{3,2,1,0:T(8,128)(2,1)S(1)}, u32[]{:S(2)}, u32[]{:S(2)}) collective-permute-start(bf16[4,1,16,320]{3,2,1,0:T(8,128)(2,1)S(1)} %get-tuple-element.3), channel_id=1, source_target_pairs={{1,0},{2,1},{3,2},{5,4},{6,5},{7,6},{9,8},{10,9},{11,10},{13,12},{... | collective-permute-start | bytes 122888 | tf_op jit(solution)/shard_map/ppermute | solution.py:18
  122.9 21.6 %copy-start.3 = (bf16[2,16,16,320]{3,2,1,0:T(8,128)(2,1)}, bf16[2,16,16,320]{3,2,1,0:T(8,128)(2,1)S(1)}, u32[]{:S(2)}) copy-start(bf16[2,16,16,320]{3,2,1,0:T(8,128)(2,1)S(1)} %fusion.16) | copy-start | bytes 983044
  123.4 12.1 %collective-permute-start.16 = (f32[16,4]{0,1:T(4,128)S(1)}, f32[16,4]{0,1:T(4,128)S(1)}, u32[]{:S(2)}, u32[]{:S(2)}) collective-permute-start(f32[16,4]{0,1:T(4,128)S(1)} %get-tuple-element.18), channel_id=1, source_target_pairs={{0,4},{4,8},{8,12},{12,16},{16,20},{20,24},{24,28},{28,32},{32,36}... | collective-permute-start | bytes 776 | tf_op jit(solution)/shard_map/ppermute | solution.py:26
  133.6 10.3 %collective-permute-start.17 = (f32[16,4]{0,1:T(4,128)S(1)}, f32[16,4]{0,1:T(4,128)S(1)}, u32[]{:S(2)}, u32[]{:S(2)}) collective-permute-start(f32[16,4]{0,1:T(4,128)S(1)} %get-tuple-element.19), channel_id=1, source_target_pairs={{4,0},{8,4},{12,8},{16,12},{20,16},{24,20},{28,24},{32,28},{36,32}... | collective-permute-start | bytes 776 | tf_op jit(solution)/shard_map/ppermute | solution.py:26
where the time goes:
time: 145 us
  starting transfers between devices  80 us (55%)
  waiting for transfers between devices  50.7 us (35%)
  matrix products  9.87 us (7%)
  local copies, waits for them, and re-layouts  1.5 us (1%)
    ppermute x8, starting transfers between devices, with_halo(): lax.ppermute(lax.slice_in_dim(block, block.shape[dim] - width, None, axis...  52.5 us
    ppermute x8, waiting for transfers between devices, with_halo(): lax.ppermute(lax.slice_in_dim(block, 0, width, axis=dim), axis, backward)  38.1 us
    ppermute x8, starting transfers between devices, with_halo(): lax.ppermute(lax.slice_in_dim(block, 0, width, axis=dim), axis, backward)  15.4 us
    ppermute x2, starting transfers between devices, passed_along(): return lax.ppermute(x, axis, pairs)  12.1 us
    dot_general x20, matrix products, couple(): lax.dot_general(field_now, matrix, dims, preferred_element_type=jnp.float32)  9.36 us
    ppermute x2, waiting for transfers between devices, passed_along(): return lax.ppermute(x, axis, pairs)  8.41 us
    ppermute x8, waiting for transfers between devices, with_halo(): lax.ppermute(lax.slice_in_dim(block, block.shape[dim] - width, None, axis...  4.2 us
  transfers between devices with their start and end apart: 18, of which 12 were waited for; matrix products, arithmetic and copies ran while one was open for 5% of the time, Pallas kernels for 0%

commit v1 on v0

v1 whole, which is shorter than its diff:
```python
import jax
import jax.numpy as jnp
from jax import lax
from jax.sharding import Mesh, PartitionSpec as P

ACT = 4096
STEPS = 2
DOF = 320
FORC = 16
RING = 4
WIDE = 384
HALO = 6
BF = jnp.bfloat16


def body(state, bits, couplings, shapes, amap):
    n_h, n_rad = lax.axis_size("h"), lax.axis_size("r")
    h, y, r = lax.axis_index("h"), lax.axis_index("y"), lax.axis_index("r")
    axb, radb = state.shape[:2]
    blocks = axb * radb
    per_group = ACT // (n_h * RING * n_rad)
    ahead = [(i, i + 1) for i in range(n_h - 1)]
    back = [(b, a) for a, b in ahead]

    edge = []
    for i in range(n_h - 1):
        edge.append((i * RING + RING - 1, (i + 1) * RING + RING - 1))
        edge.append(((i + 1) * RING, i * RING))
    beside = lax.ppermute(shapes, ("h", "y"), edge)
    vecs = lax.all_gather(jnp.stack([shapes, beside]), ("y", "r"))
    vecs = vecs.reshape(RING, n_rad, 2, axb, radb, DOF).transpose(0, 2, 3, 1, 4, 5)
    vecs = jnp.concatenate([vecs[-1:, 1], vecs[:, 0], vecs[:1, 1]], 0)
    vecs = vecs.reshape((RING + 2) * axb, n_rad * radb, DOF)

    group_of = amap // per_group
    shift = (group_of - ((h * RING + y) * n_rad + r)) // n_rad
    column = (shift + 1) * per_group + amap % per_group
    meta = jnp.concatenate([bits, column[..., None]], -1).astype(BF).reshape(1, blocks, 5)
    send = state.transpose(2, 0, 1, 3).reshape(FORC, blocks, DOF)
    send = jnp.concatenate([send, jnp.broadcast_to(meta, (FORC, blocks, 5)), jnp.zeros((FORC, blocks, WIDE - DOF - 5), BF)], -1)
    mine = lax.all_to_all(send, ("y", "r"), 0, 0, tiled=True)
    low = lax.ppermute(mine[n_rad:], "h", ahead)
    high = lax.ppermute(mine[:-n_rad], "h", back)
    window = jnp.concatenate([low, mine, high], 0)
    slabs = window.shape[0] // n_rad
    window = window.reshape(slabs, n_rad, axb, radb, WIDE).transpose(0, 2, 1, 3, 4).reshape(slabs * axb, n_rad * radb, WIDE)
    field = window[..., :DOF]
    masks = window[..., DOF : DOF + 4].astype(jnp.float32)
    column = window[..., DOF + 4].astype(jnp.int32)

    opposite = [1, 0, 3, 2]
    for step in range(2 * STEPS):
        adjoint = step >= STEPS
        dims = (((2,), (1 if adjoint else 0,)), ((), ()))
        mid = field[1:-1]
        side = jnp.pad(mid, ((0, 0), (1, 1), (0, 0)))
        near = [field[:-2], field[2:], side[:, :-2], side[:, 2:]]
        masks = masks[1:-1]
        total = lax.dot_general(mid, couplings[0], dims, preferred_element_type=jnp.float32)
        for e in range(4):
            matrix = couplings[opposite[e] + 1] if adjoint else couplings[e + 1]
            total = total + masks[:, :, e : e + 1] * lax.dot_general(near[e], matrix, dims, preferred_element_type=jnp.float32)
        field = total.astype(BF)

    cut = 2 * STEPS
    rows = field.shape[0]
    column = column[cut : cut + rows]
    proj = jnp.einsum("xyk,xyk->xy", field, vecs, preferred_element_type=jnp.float32)
    slab = jnp.arange(rows, dtype=jnp.int32)[:, None] // axb - 1
    cycle = jnp.arange(n_rad * radb, dtype=jnp.int32)[None, :] // radb
    target = ((slab + column // per_group - 1) * n_rad + cycle) * per_group + column % per_group
    hot = (target.reshape(-1, 1) == jnp.arange(RING * n_rad * per_group, dtype=jnp.int32)[None]).astype(jnp.float32)
    grad = jnp.sum(proj.reshape(-1, 1) * hot, 0).reshape(FORC, per_group)
    top = lax.reduce_precision(grad, 8, 7)
    tail = jnp.concatenate([top, grad - top], -1).astype(BF)
    tail = jnp.pad(tail[:, None], ((0, 0), (0, blocks - 1), (0, WIDE - DOF - 2 * per_group)))
    own = field[axb:-axb].reshape(RING, axb, n_rad, radb, DOF).transpose(0, 2, 1, 3, 4).reshape(FORC, blocks, DOF)
    back_home = lax.all_to_all(jnp.concatenate([own, tail], -1), ("y", "r"), 0, 0, tiled=True)
    result = back_home[..., :DOF].reshape(FORC, axb, radb, DOF).transpose(1, 2, 0, 3)
    tail = back_home[:, 0, DOF : DOF + 2 * per_group].astype(jnp.float32)
    return result, tail[:, :per_group] + tail[:, per_group:]


def solution(mesh):
    n_ax, n_rad = mesh.shape["ax"], mesh.shape["rad"]
    fine = Mesh(mesh.devices.reshape(n_ax // RING, RING, n_rad), ("h", "y", "r"))
    ax = ("h", "y")
    in_specs = (P(ax, "r"), P(ax, "r"), P(), P(ax, "r"), P(ax, "r"))
    out_specs = (P(ax, "r"), P(None, ("h", "y", "r")))
    return jax.shard_map(body, mesh=fine, in_specs=in_specs, out_specs=out_specs, check_vma=False)
```

time: 145 us -> 125 us (0.86)
  the two profiles are of different devices: /device:TPU:479 before, /device:TPU:1 now
where the time goes in v1:
time: 125 us; the launch traced here: 124 us
  blocking collectives  62 us (50%)
  starting transfers between devices  24.4 us (20%)
  matrix products  15.1 us (12%)
  local copies, waits for them, and re-layouts  9.47 us (8%)
  waiting for transfers between devices  8.27 us (7%)
  other arithmetic  4.01 us (3%)
    all_gather x1, blocking collectives, body(): vecs = lax.all_gather(jnp.stack([shapes, beside]), ('y', 'r'))  37.1 us
    all_to_all x1, blocking collectives, body(): lax.all_to_all(jnp.concatenate([own, tail], -1), ('y', 'r'), 0, 0, tiled=...  25 us
    all_to_all x1, starting transfers between devices, body(): mine = lax.all_to_all(send, ('y', 'r'), 0, 0, tiled=True)  17.5 us
    dot_general x16, matrix products, body(): lax.dot_general(near[e], matrix, dims, preferred_element_type=jnp.float32)  11.6 us
    ppermute x1, waiting for transfers between devices, body(): low = lax.ppermute(mine[n_rad:], 'h', ahead)  4.46 us
    ppermute x1, starting transfers between devices, body(): low = lax.ppermute(mine[n_rad:], 'h', ahead)  4.28 us
    slice x4, local copies, waits for them, and re-layouts, body(): masks[:, :, e:e + 1]  3.91 us
    ppermute x1, waiting for transfers between devices, body(): high = lax.ppermute(mine[:-n_rad], 'h', back)  3.81 us
  transfers between devices with their start and end apart: 4, of which 2 were waited for; matrix products, arithmetic and copies ran while one was open for 3% of the time, Pallas kernels for 0%

profile of v1, /device:TPU:1, one launch (start us, length us, event | category | flops | bytes accessed | tf_op | source)
XLA Modules:
  0.0 124.3 jit_solution(3754260230640840901)
XLA Ops:
  0.6 1.3 %collective-permute-start.2 = (bf16[2,16,320]{2,1,0:T(8,128)(2,1)}, bf16[2,16,320]{2,1,0:T(8,128)(2,1)S(1)}, u32[]{:S(2)}, u32[]{:S(2)}) collective-permute-start(bf16[2,16,320]{2,1,0:T(8,128)(2,1)} %param.8), channel_id=1, source_target_pairs={{12,28},{16,0},{28,44},{32,16},{44,60},{48,32},{60,76},{64,48},{76... | collective-permute-start | bytes 61448 | tf_op jit(solution)/shard_map/ppermute | solution.py:29
  1.9 0.7 fusion.77
  2.7 0.7 convert.19
  3.6 1.1 copy.73
  4.8 0.9 maximum_maximum_fusion
  5.7 17.5 %all-to-all-start = ((bf16[16,32,384]{2,1,0:T(8,128)(2,1)}), bf16[16,32,384]{2,1,0:T(8,128)(2,1)S(1)}, u32[]{:S(2)}, u32[]{:S(2)}) async-start(bf16[16,32,384]{2,1,0:T(8,128)(2,1)} %maximum_maximum_fusion), calls=%async_computation | async-start | bytes 786432 | tf_op jit(solution)/shard_map/all_to_all | solution.py:41
  23.3 37.1 %all-gather = bf16[32,2,16,320]{3,2,1,0:T(8,128)(2,1)S(1)} all-gather(bf16[2,2,16,320]{3,2,1,0:T(8,128)(2,1)S(1)} %pad_maximum_fusion.2), channel_id=2, replica_groups=mesh['h'=64,'y'=4,'r'=4] {'y','r'}, dimensions={0}, use_global_device_ids=true | all-gather | bytes 696320 | tf_op jit(solution)/shard_map/all_gather | solution.py:30
  60.4 4.3 %collective-permute-start = (bf16[12,32,384]{2,1,0:T(8,128)(2,1)S(1)}, bf16[12,32,384]{2,1,0:T(8,128)(2,1)S(1)}, u32[]{:S(2)}, u32[]{:S(2)}) collective-permute-start(bf16[12,32,384]{2,1,0:T(8,128)(2,1)S(1)} %get-tuple-element.20), channel_id=1, source_target_pairs={{0,16},{16,32},{32,48},{48,64},{64,80},{80,96},{96,112},{112,128},... | collective-permute-start | bytes 884744 | tf_op jit(solution)/shard_map/ppermute | solution.py:42
  64.7 1.3 %collective-permute-start.1 = (bf16[12,32,384]{2,1,0:T(8,128)(2,1)S(1)}, bf16[12,32,384]{2,1,0:T(8,128)(2,1)S(1)}, u32[]{:S(2)}, u32[]{:S(2)}) collective-permute-start(bf16[12,32,384]{2,1,0:T(8,128)(2,1)S(1)} %get-tuple-element.21), channel_id=1, source_target_pairs={{16,0},{32,16},{48,32},{64,48},{80,64},{96,80},{112,96},{128,112},... | collective-permute-start | bytes 884744 | tf_op jit(solution)/shard_map/ppermute | solution.py:43
  66.3 4.5 %collective-permute-done = bf16[12,32,384]{2,1,0:T(8,128)(2,1)S(1)} collective-permute-done((bf16[12,32,384]{2,1,0:T(8,128)(2,1)S(1)}, bf16[12,32,384]{2,1,0:T(8,128)(2,1)S(1)}, u32[]{:S(2)}, u32[]{:S(2)}) %collective-permute-start) | collective-permute-done | bytes 294944 | tf_op jit(solution)/shard_map/ppermute | solution.py:42
  70.7 3.8 %collective-permute-done.1 = bf16[12,32,384]{2,1,0:T(8,128)(2,1)S(1)} collective-permute-done((bf16[12,32,384]{2,1,0:T(8,128)(2,1)S(1)}, bf16[12,32,384]{2,1,0:T(8,128)(2,1)S(1)}, u32[]{:S(2)}, u32[]{:S(2)}) %collective-permute-start.1) | collective-permute-done | bytes 294944 | tf_op jit(solution)/shard_map/ppermute | solution.py:43
  75.4 0.8 slice_reduce_fusion.13
  76.2 0.9 slice_reduce_fusion.10
  77.1 1.0 slice_reduce_fusion.7
  78.2 1.2 slice_reduce_fusion.3
  79.4 1.2 copy-done
  83.4 1.4 %add_convert_fusion = bf16[18,64,320]{2,1,0:T(8,128)(2,1)S(1)} fusion(f32[18,64,320]{2,1,0:T(8,128)S(1)} %fusion.10, f32[18,64,320]{2,1,0:T(8,128)S(1)} %fusion.11, f32[18,64,320]{2,1,0:T(8,128)S(1)} %fusion.41, f32[18,64,320]{2,1,0:T(8,128)S(1)} %fusion.13, bf16[18,64,320]{2,1,0:T(8,128)(2,1)S(1)} %slice.267, f32[18,64]{1,0:T(8,128)S(1)} %get-tuple-element.15, ...), kind=kOutput, calls=%fused_computation | convolution fusion | flops 239247360 | bytes 8994816 | tf_op jit(solution)/shard_map/dot_general | solution.py:62
  87.4 1.4 %add_convert_fusion.1 = bf16[16,64,320]{2,1,0:T(8,128)(2,1)S(1)} fusion(f32[16,64,320]{2,1,0:T(8,128)S(1)} %fusion.16, f32[16,64,320]{2,1,0:T(8,128)S(1)} %fusion.15, f32[16,64,320]{2,1,0:T(8,128)S(1)} %fusion.39, f32[16,64,320]{2,1,0:T(8,128)S(1)} %fusion.33, bf16[18,64,320]{2,1,0:T(8,128)(2,1)S(1)} %add_convert_fusion, ...), kind=kOutput, calls=%fused_computation.1 | convolution fusion | flops 212664320 | bytes 8110080 | tf_op jit(solution)/shard_map/dot_general | solution.py:62
  88.9 1.7 %fusion.37 = f32[14,64,320]{2,1,0:T(8,128)} fusion(bf16[16,64,320]{2,1,0:T(8,128)(2,1)S(1)} %add_convert_fusion.1, bf16[5,320,320]{2,1,0:T(8,128)(2,1)S(1)} %copy-done), kind=kOutput, calls=%fused_computation.81 | convolution fusion | flops 183500800 | bytes 2179072 | tf_op jit(solution)/shard_map/dot_general | solution.py:59
  91.9 0.7 copy-done.1
  93.3 0.7 fusion.7
  96.2 0.8 fusion.9
  97.7 25.0 %all_to_all.10 = bf16[16,32,384]{2,1,0:T(8,128)(2,1)S(1)} all-to-all(bf16[16,32,384]{2,1,0:T(8,128)(2,1)S(1)} %fusion.18), channel_id=1, replica_groups=mesh['h'=64,'y'=4,'r'=4] {'y','r'}, dimensions={0} | all-to-all | bytes 786432 | tf_op jit(solution)/shard_map/all_to_all | solution.py:78
  123.5 0.9 copy.94
  (61 shorter events, 12.6 us)
Async XLA Ops:
  0.6 22.6 %copy-start.2 = (bf16[2,16,320]{2,1,0:T(8,128)(2,1)S(1)}, bf16[2,16,320]{2,1,0:T(8,128)(2,1)}, u32[]{:S(2)}) copy-start(bf16[2,16,320]{2,1,0:T(8,128)(2,1)} %param.8) | copy-start | bytes 61444
  0.6 22.6 %collective-permute-start.2 = (bf16[2,16,320]{2,1,0:T(8,128)(2,1)}, bf16[2,16,320]{2,1,0:T(8,128)(2,1)S(1)}, u32[]{:S(2)}, u32[]{:S(2)}) collective-permute-start(bf16[2,16,320]{2,1,0:T(8,128)(2,1)} %param.8), channel_id=1, source_target_pairs={{12,28},{16,0},{28,44},{32,16},{44,60},{48,32},{60,76},{64,48},{76... | collective-permute-start | bytes 61448 | tf_op jit(solution)/shard_map/ppermute | solution.py:29
  5.7 54.7 %all-to-all-start = ((bf16[16,32,384]{2,1,0:T(8,128)(2,1)}), bf16[16,32,384]{2,1,0:T(8,128)(2,1)S(1)}, u32[]{:S(2)}, u32[]{:S(2)}) async-start(bf16[16,32,384]{2,1,0:T(8,128)(2,1)} %maximum_maximum_fusion), calls=%async_computation | async-start | bytes 786432 | tf_op jit(solution)/shard_map/all_to_all | solution.py:41
  60.4 10.3 %collective-permute-start = (bf16[12,32,384]{2,1,0:T(8,128)(2,1)S(1)}, bf16[12,32,384]{2,1,0:T(8,128)(2,1)S(1)}, u32[]{:S(2)}, u32[]{:S(2)}) collective-permute-start(bf16[12,32,384]{2,1,0:T(8,128)(2,1)S(1)} %get-tuple-element.20), channel_id=1, source_target_pairs={{0,16},{16,32},{32,48},{48,64},{64,80},{80,96},{96,112},{112,128},... | collective-permute-start | bytes 884744 | tf_op jit(solution)/shard_map/ppermute | solution.py:42
  64.7 9.8 %collective-permute-start.1 = (bf16[12,32,384]{2,1,0:T(8,128)(2,1)S(1)}, bf16[12,32,384]{2,1,0:T(8,128)(2,1)S(1)}, u32[]{:S(2)}, u32[]{:S(2)}) collective-permute-start(bf16[12,32,384]{2,1,0:T(8,128)(2,1)S(1)} %get-tuple-element.21), channel_id=1, source_target_pairs={{16,0},{32,16},{48,32},{64,48},{80,64},{96,80},{112,96},{128,112},... | collective-permute-start | bytes 884744 | tf_op jit(solution)/shard_map/ppermute | solution.py:43
  79.3 1.3 %copy-start = (bf16[5,320,320]{2,1,0:T(8,128)(2,1)S(1)}, bf16[5,320,320]{2,1,0:T(8,128)(2,1)}, u32[]{:S(2)}) copy-start(bf16[5,320,320]{2,1,0:T(8,128)(2,1)} %param.7) | copy-start | bytes 3072004
  91.3 1.3 %copy-start.1 = (f32[14,64,320]{2,1,0:T(8,128)S(1)}, f32[14,64,320]{2,1,0:T(8,128)}, u32[]{:S(2)}) copy-start(f32[14,64,320]{2,1,0:T(8,128)} %fusion.37) | copy-start | bytes 3440644

commit v2 on v1

v2 whole, which is shorter than its diff:
```python
import functools

import jax
import jax.numpy as jnp
from jax import lax
from jax.experimental import pallas as pl
from jax.experimental.pallas import tpu as pltpu
from jax.sharding import Mesh, PartitionSpec as P

ACT = 4096
STEPS = 2
DOF = 320
FORC = 16
RING = 4
AXB = 2
RADB = 16
BLOCKS = AXB * RADB
WIDE = 384
MAIN = 256
HALO = 2 * STEPS
BF = jnp.bfloat16
F32 = jnp.float32
ROWS = FORC * BLOCKS
NRAD = 4
LINE = NRAD * RADB
WINDOW = RING * AXB + 2 * HALO
DEPTH = 5 * MAIN + WIDE
PACKED = 80


def iota(shape, dim):
    return lax.broadcasted_iota(jnp.int32, shape, dim)


def one_hot(rows, cols, of_row):
    return jnp.where(iota((rows, cols), 1) == of_row(iota((rows, cols), 0)), 1.0, 0.0).astype(BF)


def dot(a, b):
    return jnp.dot(a, b, preferred_element_type=F32)


def pack_kernel(state_ref, bits_ref, out_ref, wide):
    wide[...] = jnp.zeros_like(wide)
    wide[:, :DOF] = state_ref[...]
    order = one_hot(ROWS, ROWS, lambda o: (o % BLOCKS) * FORC + o // BLOCKS)
    block = one_hot(ROWS, BLOCKS, lambda o: o % BLOCKS)
    out = dot(order, wide[...]) + dot(block, bits_ref[...])
    out_ref[...] = out.astype(BF).reshape(FORC, BLOCKS, WIDE)


def pack(state, bits):
    return pl.pallas_call(
        pack_kernel,
        out_shape=jax.ShapeDtypeStruct((FORC, BLOCKS, WIDE), BF),
        scratch_shapes=[pltpu.VMEM((ROWS, WIDE), BF)],
        compiler_params=pltpu.CompilerParams(vmem_limit_bytes=32 * 1024 * 1024),
        name="pack",
    )(state, bits)


def steps_kernel(low_ref, mine_ref, high_ref, fore_ref, adj_ref, out_ref, s_a, s_b, left, right, masks):
    total = WINDOW * LINE
    for i in range(WINDOW):
        for r in range(NRAD):
            if i < HALO:
                ref, at = low_ref, i
            elif i < WINDOW - HALO:
                ref, at = mine_ref, i - HALO
            else:
                ref, at = high_ref, i - (WINDOW - HALO)
            slot, half = (at // AXB) * NRAD + r, at % AXB
            row = i * LINE + r * RADB
            s_a[row : row + RADB, :] = ref[slot, half * RADB : (half + 1) * RADB, :]
    pick = jnp.where(iota((128, 512), 0) == 64 + iota((128, 512), 1) // 128, 1.0, 0.0).astype(BF)
    spread = dot(s_a[:, MAIN:], pick)
    place = iota((total, 128), 0) % LINE
    masks[:, :256] = spread[:, :256].astype(BF)
    masks[:, 256:384] = jnp.where(place > 0, spread[:, 256:384], 0.0).astype(BF)
    masks[:, 384:] = jnp.where(place < LINE - 1, spread[:, 384:], 0.0).astype(BF)
    tail = s_a[:, MAIN:].astype(F32)
    tail = jnp.where(iota((total, 128), 1) < 64, tail, pltpu.roll(tail, 64, 1))
    s_a[:, MAIN:] = tail.astype(BF)

    def sides(value, a, b):
        down, up = pltpu.roll(value, 1, 0).astype(BF), pltpu.roll(value, b - a - 1, 0).astype(BF)
        for t in range(3):
            cols = slice(128 * t, 128 * t + 128)
            left[a:b, cols] = down[:, cols] * masks[a:b, 256:384]
            right[a:b, cols] = up[:, cols] * masks[a:b, 384:]

    a, b = LINE, total - LINE
    for c in range(a, b, 7 * LINE):
        sides(s_a[c : c + 7 * LINE, :].astype(F32), c, c + 7 * LINE)

    now, later = s_a, s_b
    for step in range(2 * STEPS):
        weights = fore_ref if step < STEPS else adj_ref
        first, last = step + 1, WINDOW - step - 1
        chunk = (last - first) // 2
        for i in range(first, last, chunk):
            a, b = i * LINE, (i + chunk) * LINE
            first_half = iota((b - a, 128), 1) < 64
            m0, m1 = masks[a:b, :128], masks[a:b, 128:256]
            prev, own, nxt = now[a - LINE : b - LINE, :], now[a:b, :], now[a + LINE : b + LINE, :]
            lhs = jnp.concatenate(
                [
                    own[:, :MAIN],
                    prev[:, :128] * m0,
                    prev[:, 128:256] * m0,
                    nxt[:, :128] * m1,
                    nxt[:, 128:256] * m1,
                    left[a:b, :MAIN],
                    right[a:b, :MAIN],
                    jnp.where(first_half, own[:, MAIN:], prev[:, MAIN:] * m0),
                    jnp.where(first_half, nxt[:, MAIN:] * m1, left[a:b, MAIN:]),
                    right[a:b, MAIN:],
                ],
                axis=1,
            )
            value = dot(lhs, weights[...])
            later[a:b, :] = value.astype(BF)
            if step < 2 * STEPS - 1:
                sides(value, a, b)
        now, later = later, now

    early = iota((RADB, 128), 1) < 64
    for y in range(RING):
        for r in range(NRAD):
            rows = [(HALO + y * AXB + half) * LINE + r * RADB for half in range(AXB)]
            slot = y * NRAD + r
            for half, row in enumerate(rows):
                out_ref[slot, half * RADB : (half + 1) * RADB, :] = now[row : row + RADB, :128]
                out_ref[slot, BLOCKS + half * RADB : BLOCKS + (half + 1) * RADB, :] = now[row : row + RADB, 128:256]
            out_ref[slot, 2 * BLOCKS :, :] = jnp.where(early, now[rows[0] : rows[0] + RADB, MAIN:], now[rows[1] : rows[1] + RADB, MAIN:])


def steps(low, mine, high, fore, adj):
    field = pltpu.VMEM((WINDOW * LINE, WIDE), BF)
    return pl.pallas_call(
        steps_kernel,
        out_shape=jax.ShapeDtypeStruct((FORC, PACKED, 128), BF),
        scratch_shapes=[field, field, field, field, pltpu.VMEM((WINDOW * LINE, 512), BF)],
        compiler_params=pltpu.CompilerParams(vmem_limit_bytes=48 * 1024 * 1024),
        name="steps",
    )(low, mine, high, fore, adj)


def unpack_kernel(back_ref, shapes_ref, hot_ref, state_ref, prev_ref, own_ref, next_ref, wide):
    for f in range(FORC):
        row = f * BLOCKS
        wide[row : row + BLOCKS, :128] = back_ref[f, :BLOCKS, :]
        wide[row : row + BLOCKS, 128:256] = back_ref[f, BLOCKS : 2 * BLOCKS, :]
        tail = back_ref[f, 2 * BLOCKS :, :]
        wide[row : row + RADB, MAIN:] = tail
        wide[row + RADB : row + BLOCKS, MAIN:] = pltpu.roll(tail.astype(F32), 64, 1).astype(BF)
    order = one_hot(ROWS, ROWS, lambda o: (o % FORC) * BLOCKS + o // FORC)
    state = dot(order, wide[...])[:, :DOF]
    state_ref[...] = state.astype(BF)
    block = one_hot(ROWS, BLOCKS, lambda o: o // FORC)
    proj = jnp.sum(state * dot(block, shapes_ref[...]), axis=1, keepdims=True)
    part = proj * dot(block, hot_ref[...])
    part = jnp.sum(part.reshape(BLOCKS, FORC, 128), axis=0)
    prev_ref[...] = part[:, 0:4]
    own_ref[...] = part[:, 4:8]
    next_ref[...] = part[:, 8:12]


def unpack(back, shapes, hot):
    part = jax.ShapeDtypeStruct((FORC, 4), F32)
    return pl.pallas_call(
        unpack_kernel,
        out_shape=(jax.ShapeDtypeStruct((ROWS, DOF), BF), part, part, part),
        scratch_shapes=[pltpu.VMEM((ROWS, WIDE), BF)],
        compiler_params=pltpu.CompilerParams(vmem_limit_bytes=32 * 1024 * 1024),
        name="unpack",
    )(back, shapes, hot)


def stacked(matrices):
    rows = jnp.concatenate(
        [m[:MAIN] for m in matrices] + [m[MAIN:] for m in matrices] + [jnp.zeros((64, DOF), BF)], axis=0
    )
    return jnp.concatenate([rows, rows[:, MAIN:]], axis=1)


def body(state, bits, couplings, shapes, amap):
    n_h, n_rad = lax.axis_size("h"), lax.axis_size("r")
    h, y, r = lax.axis_index("h"), lax.axis_index("y"), lax.axis_index("r")
    per_group = ACT // (n_h * RING * n_rad)
    ahead = [(i, i + 1) for i in range(n_h - 1)]
    back = [(b, a) for a, b in ahead]

    bits = jnp.pad(bits.reshape(BLOCKS, 4).astype(BF), ((0, 0), (DOF, WIDE - DOF - 4)))
    send = pack(state.reshape(ROWS, DOF), bits)
    mine = lax.all_to_all(send, ("y", "r"), 0, 0, tiled=True)
    reach = HALO // AXB * n_rad
    low = lax.ppermute(mine[-reach:], "h", ahead)
    high = lax.ppermute(mine[:reach], "h", back)

    fore = stacked([couplings[e] for e in range(5)])
    adj = stacked([couplings[e].T for e in (0, 2, 1, 4, 3)])
    out = steps(low, mine, high, fore, adj)
    back_home = lax.all_to_all(out, ("y", "r"), 0, 0, tiled=True)

    amap = amap.reshape(BLOCKS, 1)
    shift = (amap // per_group - ((h * RING + y) * n_rad + r)) // n_rad
    column = (shift + 1) * per_group + amap % per_group
    hot = (column == jnp.arange(128, dtype=jnp.int32)[None, :]).astype(BF)
    result, to_prev, own, to_next = unpack(back_home, shapes.reshape(BLOCKS, DOF), hot)
    n_ax = n_h * RING
    up = [(i, i + 1) for i in range(n_ax - 1)]
    from_prev = lax.ppermute(to_next, ("h", "y"), up)
    from_next = lax.ppermute(to_prev, ("h", "y"), [(b, a) for a, b in up])
    return result.reshape(state.shape), own + from_prev + from_next


def solution(mesh):
    n_ax, n_rad = mesh.shape["ax"], mesh.shape["rad"]
    fine = Mesh(mesh.devices.reshape(n_ax // RING, RING, n_rad), ("h", "y", "r"))
    ax = ("h", "y")
    in_specs = (P(ax, "r"), P(ax, "r"), P(), P(ax, "r"), P(ax, "r"))
    out_specs = (P(ax, "r"), P(None, ("h", "y", "r")))
    return jax.shard_map(body, mesh=fine, in_specs=in_specs, out_specs=out_specs, check_vma=False)
```

time: 125 us -> 91.1 us (0.73)
  the two profiles are of different devices: /device:TPU:1 before, /device:TPU:479 now
where the time goes in v2:
time: 91.1 us; the launch traced here: 89.4 us
  starting transfers between devices  28.9 us (32%)
  waiting for transfers between devices  25.6 us (28%)
  local copies, waits for them, and re-layouts  21.8 us (24%)
  Pallas kernels  9.6 us (11%)
  other arithmetic  2.64 us (3%)
    unnamed x36, local copies, waits for them, and re-layouts  18.8 us
    all_to_all x1, waiting for transfers between devices, body(): back_home = lax.all_to_all(out, ('y', 'r'), 0, 0, tiled=True)  9.87 us
    ppermute x1, waiting for transfers between devices, body(): from_next = lax.ppermute(to_prev, ('h', 'y'), [(b, a) for a, b in up])  8.47 us
    all_to_all x1, starting transfers between devices, body(): back_home = lax.all_to_all(out, ('y', 'r'), 0, 0, tiled=True)  8.37 us
    all_to_all x1, starting transfers between devices, body(): mine = lax.all_to_all(send, ('y', 'r'), 0, 0, tiled=True)  7.65 us
    ppermute x1, waiting for transfers between devices, body(): high = lax.ppermute(mine[:reach], 'h', back)  7.12 us
    pallas_call x1, Pallas kernels, steps(): pl.pallas_call(steps_kernel, out_shape=jax.ShapeDtypeStruct((FORC, PACKED...  7.05 us
    ppermute x1, starting transfers between devices, body(): low = lax.ppermute(mine[-reach:], 'h', ahead)  5.13 us
  transfers between devices with their start and end apart: 6, of which 4 were waited for; matrix products, arithmetic and copies ran while one was open for 24% of the time, Pallas kernels for 0%

profile of v2, /device:TPU:479, one launch (start us, length us, event | category | flops | bytes accessed | tf_op | source)
XLA Modules:
  0.0 89.4 jit_solution(17621068993323772808)
XLA Ops:
  2.5 1.3 %pack.1 = bf16[16,32,384]{2,1,0:T(8,128)(2,1)} custom-call(bf16[512,320]{1,0:T(8,128)(2,1)S(1)} %bitcast.39, bf16[32,384]{1,0:T(8,128)(2,1)S(1)} %pad.4.bits_ref), custom_call_target="tpu_custom_call" | custom-call | tf_op jit(solution)/shard_map/pack/pallas_call | solution.py:53
  3.8 7.7 %all-to-all-start = ((bf16[16,32,384]{2,1,0:T(8,128)(2,1)}), bf16[16,32,384]{2,1,0:T(8,128)(2,1)S(1)}, u32[]{:S(2)}, u32[]{:S(2)}) async-start(bf16[16,32,384]{2,1,0:T(8,128)(2,1)} %pack.1), calls=%async_computation | async-start | bytes 786432 | tf_op jit(solution)/shard_map/all_to_all | solution.py:196
  11.4 1.0 %fusion.2 = (bf16[1,320,320]{2,1,0:T(8,128)(2,1)}, bf16[1,320,320]{2,1,0:T(8,128)(2,1)S(1)}, bf16[1,320,320]{2,1,0:T(8,128)(2,1)}, bf16[1,320,320]{2,1,0:T(8,128)(2,1)}, bf16[1,320,320]{2,1,0:T(8,128)(2,1)}) fusion(bf16[5,320,320]{2,1,0:T(8,128)(2,1)S(1)} %copy-done.2), kind=kLoop, calls=%fused_computation.37 | loop fusion | bytes 2048000 | tf_op jit(solution)/shard_map/slice | solution.py:201
  12.5 1.1 %copy.17 = bf16[1,320,320]{1,2,0:T(8,128)(2,1)S(1)} copy(bf16[1,320,320]{2,1,0:T(8,128)(2,1)} %get-tuple-element.16) | data formatting | bytes 409600
  14.4 1.8 %copy.18 = bf16[1,320,320]{1,2,0:T(8,128)(2,1)} copy(bf16[1,320,320]{2,1,0:T(8,128)(2,1)} %get-tuple-element.15) | data formatting | bytes 409600
  16.2 1.8 %copy.19 = bf16[1,320,320]{1,2,0:T(8,128)(2,1)} copy(bf16[1,320,320]{2,1,0:T(8,128)(2,1)} %get-tuple-element.14) | data formatting | bytes 409600
  18.2 1.1 %copy.21 = bf16[1,320,320]{1,2,0:T(8,128)(2,1)S(1)} copy(bf16[1,320,320]{2,1,0:T(8,128)(2,1)} %get-tuple-element.12) | data formatting | bytes 409600
  19.3 1.6 %slice_dynamic-update-slice_fusion.3 = bf16[1664,320]{1,0:T(8,128)(2,1)} fusion(bf16[1664,320]{1,0:T(8,128)(2,1)} %slice_dynamic-update-slice_fusion.4, bf16[320,320]{1,0:T(8,128)(2,1)} %bitcast.49), kind=kLoop, calls=%fused_computation.5 | loop fusion | bytes 393216
  20.9 1.6 %slice_dynamic-update-slice_fusion.2 = bf16[1664,320]{1,0:T(8,128)(2,1)} fusion(bf16[1664,320]{1,0:T(8,128)(2,1)} %slice_dynamic-update-slice_fusion.3, bf16[320,320]{1,0:T(8,128)(2,1)} %bitcast.45), kind=kLoop, calls=%fused_computation.4 | loop fusion | bytes 393216
  24.0 1.4 %slice_dynamic-update-slice_fusion.9 = bf16[1664,320]{1,0:T(8,128)(2,1)} fusion(bf16[1664,320]{1,0:T(8,128)(2,1)} %slice_dynamic-update-slice_fusion, bf16[320,320]{1,0:T(8,128)(2,1)} %bitcast.48), kind=kLoop, calls=%fused_computation.16 | loop fusion | bytes 98304
  25.4 1.4 %slice_dynamic-update-slice_fusion.8 = bf16[1664,320]{1,0:T(8,128)(2,1)} fusion(bf16[1664,320]{1,0:T(8,128)(2,1)} %slice_dynamic-update-slice_fusion.9, bf16[320,320]{1,0:T(8,128)(2,1)} %bitcast.50), kind=kLoop, calls=%fused_computation.15 | loop fusion | bytes 98304
  26.8 1.4 %slice_dynamic-update-slice_fusion.7 = bf16[1664,320]{1,0:T(8,128)(2,1)} fusion(bf16[1664,320]{1,0:T(8,128)(2,1)} %slice_dynamic-update-slice_fusion.8, bf16[320,320]{1,0:T(8,128)(2,1)} %bitcast.46), kind=kLoop, calls=%fused_computation.14 | loop fusion | bytes 98304
  30.1 1.0 %slice.184 = bf16[1664,64]{1,0:T(8,128)(2,1)S(1)} slice(bf16[1664,320]{1,0:T(8,128)(2,1)} %constant_dynamic-update-slice_fusion.1), slice={[0:1664], [256:320]} | slice | bytes 425984 | tf_op jit(solution)/shard_map/slice | solution.py:184
  31.5 5.1 %collective-permute-start = (bf16[8,32,384]{2,1,0:T(8,128)(2,1)S(1)}, bf16[8,32,384]{2,1,0:T(8,128)(2,1)S(1)}, u32[]{:S(2)}, u32[]{:S(2)}) collective-permute-start(bf16[8,32,384]{2,1,0:T(8,128)(2,1)S(1)} %get-tuple-element.18), channel_id=1, source_target_pairs={{0,16},{16,32},{32,48},{48,64},{64,80},{80,96},{96,112},{112,128},... | collective-permute-start | bytes 589832 | tf_op jit(solution)/shard_map/ppermute | solution.py:198
  36.6 1.9 %collective-permute-start.1 = (bf16[8,32,384]{2,1,0:T(8,128)(2,1)S(1)}, bf16[8,32,384]{2,1,0:T(8,128)(2,1)S(1)}, u32[]{:S(2)}, u32[]{:S(2)}) collective-permute-start(bf16[8,32,384]{2,1,0:T(8,128)(2,1)S(1)} %get-tuple-element.17), channel_id=1, source_target_pairs={{16,0},{32,16},{48,32},{64,48},{80,64},{96,80},{112,96},{128,112},... | collective-permute-start | bytes 589832 | tf_op jit(solution)/shard_map/ppermute | solution.py:199
  38.5 1.8 %pad_maximum_fusion = (bf16[1664,384]{1,0:T(8,128)(2,1)S(1)}, bf16[1664,384]{1,0:T(8,128)(2,1)S(1)}) fusion(bf16[1664,64]{1,0:T(8,128)(2,1)S(1)} %slice.173, bf16[1664,320]{1,0:T(8,128)(2,1)S(1)} %constant_dynamic-update-slice_fusion, bf16[1664,64]{1,0:T(8,128)(2,1)S(1)} %slice.184, bf16[1664,320]{1,0:T(8,128)(2,1)} %constant_dynamic-update-slice_fusion.1), kind=kLoop, calls=%fused_computation | loop fusion | flops 5111808 | bytes 5111808 | tf_op jit(solution)/shard_map/concatenate | solution.py:184
  40.5 7.1 %collective-permute-done.1.high_ref = bf16[8,32,384]{2,1,0:T(8,128)(2,1)S(1)} collective-permute-done((bf16[8,32,384]{2,1,0:T(8,128)(2,1)S(1)}, bf16[8,32,384]{2,1,0:T(8,128)(2,1)S(1)}, u32[]{:S(2)}, u32[]{:S(2)}) %collective-permute-start.1) | collective-permute-done | bytes 196640 | tf_op jit(solution)/shard_map/ppermute | solution.py:199
  47.6 7.0 %steps.1 = bf16[16,80,128]{2,1,0:T(8,128)(2,1)} custom-call(bf16[8,32,384]{2,1,0:T(8,128)(2,1)S(1)} %collective-permute-done.low_ref, bf16[16,32,384]{2,1,0:T(8,128)(2,1)S(1)} %all-to-all-done.mine_ref, bf16[8,32,384]{2,1,0:T(8,128)(2,1)S(1)} %collective-permute-done.1.high_ref, bf16[1664,384]{1,0:T(8,128)(2,1)S(1)} %get-tuple-element.19.fore_ref, ...), custom_call_target="tpu_custom_call" | custom-call | tf_op jit(solution)/shard_map/steps/pallas_call | solution.py:140
  54.7 8.4 %all-to-all-start.1 = ((bf16[16,80,128]{2,1,0:T(8,128)(2,1)}), bf16[16,80,128]{2,1,0:T(8,128)(2,1)S(1)}, u32[]{:S(2)}, u32[]{:S(2)}) async-start(bf16[16,80,128]{2,1,0:T(8,128)(2,1)} %steps.1), calls=%async_computation.1 | async-start | bytes 655360 | tf_op jit(solution)/shard_map/all_to_all | solution.py:204
  63.2 9.9 %all-to-all-done.1.back_ref = bf16[16,80,128]{2,1,0:T(8,128)(2,1)S(1)} async-done(((bf16[16,80,128]{2,1,0:T(8,128)(2,1)}), bf16[16,80,128]{2,1,0:T(8,128)(2,1)S(1)}, u32[]{:S(2)}, u32[]{:S(2)}) %all-to-all-start.1) | async-done | bytes 327712 | tf_op jit(solution)/shard_map/all_to_all | solution.py:204
  73.1 1.3 %unpack.1 = (bf16[512,320]{1,0:T(8,128)(2,1)}, f32[16,4]{1,0:T(8,128)S(1)}, f32[16,4]{1,0:T(8,128)S(1)}, f32[16,4]{1,0:T(8,128)S(1)}) custom-call(bf16[16,80,128]{2,1,0:T(8,128)(2,1)S(1)} %all-to-all-done.1.back_ref, bf16[32,320]{1,0:T(8,128)(2,1)S(1)} %bitcast.40, bf16[32,128]{1,0:T(8,128)(2,1)S(1)} %fusion.hot_ref), custom_call_target="tpu_custom_call" | custom-call | tf_op jit(solution)/shard_map/unpack/pallas_call | solution.py:171
  74.4 3.9 %collective-permute-start.2 = (f32[16,4]{1,0:T(8,128)S(1)}, f32[16,4]{1,0:T(8,128)S(1)}, u32[]{:S(2)}, u32[]{:S(2)}) collective-permute-start(f32[16,4]{1,0:T(8,128)S(1)} %get-tuple-element.8), channel_id=1, source_target_pairs={{0,4},{4,8},{8,12},{12,16},{16,20},{20,24},{24,28},{28,32},{32,36}... | collective-permute-start | bytes 776 | tf_op jit(solution)/shard_map/ppermute | solution.py:213
  78.3 1.9 %collective-permute-start.3 = (f32[16,4]{1,0:T(8,128)S(1)}, f32[16,4]{1,0:T(8,128)S(1)}, u32[]{:S(2)}, u32[]{:S(2)}) collective-permute-start(f32[16,4]{1,0:T(8,128)S(1)} %get-tuple-element.9), channel_id=1, source_target_pairs={{4,0},{8,4},{12,8},{16,12},{20,16},{24,20},{28,24},{32,28},{36,32}... | collective-permute-start | bytes 776 | tf_op jit(solution)/shard_map/ppermute | solution.py:214
  80.3 8.5 %collective-permute-done.3 = f32[16,4]{1,0:T(8,128)S(1)} collective-permute-done((f32[16,4]{1,0:T(8,128)S(1)}, f32[16,4]{1,0:T(8,128)S(1)}, u32[]{:S(2)}, u32[]{:S(2)}) %collective-permute-start.3) | collective-permute-done | bytes 288 | tf_op jit(solution)/shard_map/ppermute | solution.py:214
  (41 shorter events, 7.4 us)
Async XLA Ops:
  1.5 1.0 %copy-start = (bf16[2,16,16,320]{3,2,1,0:T(8,128)(2,1)S(1)}, bf16[2,16,16,320]{3,2,1,0:T(8,128)(2,1)}, u32[]{:S(2)}) copy-start(bf16[2,16,16,320]{3,2,1,0:T(8,128)(2,1)} %param.5) | copy-start | bytes 983044
  2.5 8.9 %copy-start.2 = (bf16[5,320,320]{2,1,0:T(8,128)(2,1)S(1)}, bf16[5,320,320]{2,1,0:T(8,128)(2,1)}, u32[]{:S(2)}) copy-start(bf16[5,320,320]{2,1,0:T(8,128)(2,1)} %param.7) | copy-start | bytes 3072004
  3.8 27.6 %all-to-all-start = ((bf16[16,32,384]{2,1,0:T(8,128)(2,1)}), bf16[16,32,384]{2,1,0:T(8,128)(2,1)S(1)}, u32[]{:S(2)}, u32[]{:S(2)}) async-start(bf16[16,32,384]{2,1,0:T(8,128)(2,1)} %pack.1), calls=%async_computation | async-start | bytes 786432 | tf_op jit(solution)/shard_map/all_to_all | solution.py:196
  13.6 4.3 %copy-start.3 = (bf16[1,320,320]{1,2,0:T(8,128)(2,1)}, bf16[1,320,320]{1,2,0:T(8,128)(2,1)S(1)}, u32[]{:S(2)}) copy-start(bf16[1,320,320]{1,2,0:T(8,128)(2,1)S(1)} %copy.17) | copy-start | bytes 614404
  31.5 9.0 %collective-permute-start = (bf16[8,32,384]{2,1,0:T(8,128)(2,1)S(1)}, bf16[8,32,384]{2,1,0:T(8,128)(2,1)S(1)}, u32[]{:S(2)}, u32[]{:S(2)}) collective-permute-start(bf16[8,32,384]{2,1,0:T(8,128)(2,1)S(1)} %get-tuple-element.18), channel_id=1, source_target_pairs={{0,16},{16,32},{32,48},{48,64},{64,80},{80,96},{96,112},{112,128},... | collective-permute-start | bytes 589832 | tf_op jit(solution)/shard_map/ppermute | solution.py:198
  36.6 11.0 %collective-permute-start.1 = (bf16[8,32,384]{2,1,0:T(8,128)(2,1)S(1)}, bf16[8,32,384]{2,1,0:T(8,128)(2,1)S(1)}, u32[]{:S(2)}, u32[]{:S(2)}) collective-permute-start(bf16[8,32,384]{2,1,0:T(8,128)(2,1)S(1)} %get-tuple-element.17), channel_id=1, source_target_pairs={{16,0},{32,16},{48,32},{64,48},{80,64},{96,80},{112,96},{128,112},... | collective-permute-start | bytes 589832 | tf_op jit(solution)/shard_map/ppermute | solution.py:199
  47.6 15.4 %copy-start.4 = (s32[2,16]{1,0:T(2,128)S(1)}, s32[2,16]{1,0:T(2,128)}, u32[]{:S(2)}) copy-start(s32[2,16]{1,0:T(2,128)} %param.9) | copy-start | bytes 388
  47.6 25.5 %copy-start.1 = (bf16[2,16,320]{2,1,0:T(8,128)(2,1)S(1)}, bf16[2,16,320]{2,1,0:T(8,128)(2,1)}, u32[]{:S(2)}) copy-start(bf16[2,16,320]{2,1,0:T(8,128)(2,1)} %param.8) | copy-start | bytes 61444
  54.7 18.4 %all-to-all-start.1 = ((bf16[16,80,128]{2,1,0:T(8,128)(2,1)}), bf16[16,80,128]{2,1,0:T(8,128)(2,1)S(1)}, u32[]{:S(2)}, u32[]{:S(2)}) async-start(bf16[16,80,128]{2,1,0:T(8,128)(2,1)} %steps.1), calls=%async_computation.1 | async-start | bytes 655360 | tf_op jit(solution)/shard_map/all_to_all | solution.py:204
  74.4 5.9 %collective-permute-start.2 = (f32[16,4]{1,0:T(8,128)S(1)}, f32[16,4]{1,0:T(8,128)S(1)}, u32[]{:S(2)}, u32[]{:S(2)}) collective-permute-start(f32[16,4]{1,0:T(8,128)S(1)} %get-tuple-element.8), channel_id=1, source_target_pairs={{0,4},{4,8},{8,12},{12,16},{16,20},{20,24},{24,28},{28,32},{32,36}... | collective-permute-start | bytes 776 | tf_op jit(solution)/shard_map/ppermute | solution.py:213
  78.3 10.4 %collective-permute-start.3 = (f32[16,4]{1,0:T(8,128)S(1)}, f32[16,4]{1,0:T(8,128)S(1)}, u32[]{:S(2)}, u32[]{:S(2)}) collective-permute-start(f32[16,4]{1,0:T(8,128)S(1)} %get-tuple-element.9), channel_id=1, source_target_pairs={{4,0},{8,4},{12,8},{16,12},{20,16},{24,20},{28,24},{32,28},{36,32}... | collective-permute-start | bytes 776 | tf_op jit(solution)/shard_map/ppermute | solution.py:214

commit v3 on v2

v3 whole, which is shorter than its diff:
```python
import jax
import jax.numpy as jnp
from jax import lax
from jax.experimental import pallas as pl
from jax.experimental.pallas import tpu as pltpu
from jax.sharding import Mesh, PartitionSpec as P

ACT = 4096
STEPS = 2
DOF = 320
FORC = 16
RING = 4
AXB = 2
RADB = 16
BLOCKS = AXB * RADB
WIDE = 384
MAIN = 256
HALO = 2 * STEPS
BF = jnp.bfloat16
F32 = jnp.float32
ROWS = FORC * BLOCKS
NRAD = 4
LINE = NRAD * RADB
WINDOW = RING * AXB + 2 * HALO
DEPTH = 5 * MAIN + WIDE
PACKED = 80


def iota(shape, dim):
    return lax.broadcasted_iota(jnp.int32, shape, dim)


def one_hot(rows, cols, of_row):
    return jnp.where(iota((rows, cols), 1) == of_row(iota((rows, cols), 0)), 1.0, 0.0).astype(BF)


def dot(a, b):
    return jnp.dot(a, b, preferred_element_type=F32)


def dot_nt(a, b):
    return lax.dot_general(a, b, (((1,), (1,)), ((), ())), preferred_element_type=F32)


def call(kernel, out_shape, scratch_shapes, name, mib, flops, in_specs=None):
    return pl.pallas_call(
        kernel,
        out_shape=out_shape,
        **({} if in_specs is None else {"in_specs": in_specs}),
        scratch_shapes=scratch_shapes,
        compiler_params=pltpu.CompilerParams(vmem_limit_bytes=mib * 1024 * 1024),
        cost_estimate=pl.CostEstimate(flops=flops, bytes_accessed=2 * 1024 * 1024, transcendentals=0),
        name=name,
    )


def pack_kernel(state_ref, bits_ref, out_ref, rows, wide, bits, sem):
    copy = pltpu.make_async_copy(state_ref, rows, sem)
    copy.start()
    order = one_hot(ROWS, ROWS, lambda o: (o % BLOCKS) * FORC + o // BLOCKS)
    bits[...] = jnp.zeros_like(bits)
    for a in range(AXB):
        bits[a, 64:68, :RADB] = bits_ref[a].astype(F32)
    spread = [dot_nt(one_hot(ROWS, 128, lambda o: o % BLOCKS - a * RADB), bits[a].astype(BF)) for a in range(AXB)]
    wide[:, MAIN:] = jnp.zeros((ROWS, 128), BF)
    copy.wait()
    wide[:, :DOF] = rows[...]
    out = dot(order, wide[...]).astype(BF)
    meta = (spread[0] + spread[1]).astype(BF)
    out_ref[:, :, :MAIN] = out[:, :MAIN].reshape(FORC, BLOCKS, MAIN)
    out_ref[:, :, MAIN:] = (out[:, MAIN:] + meta).reshape(FORC, BLOCKS, 128)


def pack(state, bits):
    return call(
        pack_kernel,
        jax.ShapeDtypeStruct((FORC, BLOCKS, WIDE), BF),
        [pltpu.VMEM((ROWS, DOF), BF), pltpu.VMEM((ROWS, WIDE), BF), pltpu.VMEM((AXB, 128, 128), F32), pltpu.SemaphoreType.DMA],
        "pack",
        16,
        2 * ROWS * ROWS * WIDE,
        [pl.BlockSpec(memory_space=pl.ANY), pl.BlockSpec(memory_space=pltpu.VMEM)],
    )(state, bits)


def weights_kernel(couplings_ref, fore_ref, adj_ref):
    twice = jnp.where(
        (iota((DOF, WIDE), 1) == iota((DOF, WIDE), 0)) | (iota((DOF, WIDE), 1) == iota((DOF, WIDE), 0) + 64)
        & (iota((DOF, WIDE), 1) >= DOF),
        1.0,
        0.0,
    ).astype(BF)
    same = one_hot(DOF, DOF, lambda o: o)

    def put(ref, at, value):
        ref[at * MAIN : (at + 1) * MAIN, :] = value[:MAIN].astype(BF)
        ref[5 * MAIN + at * 64 : 5 * MAIN + (at + 1) * 64, :] = value[MAIN:].astype(BF)

    for at in range(5):
        put(fore_ref, at, dot(couplings_ref[at], twice))
    for at, e in enumerate((0, 2, 1, 4, 3)):
        matrix = couplings_ref[e]
        put(adj_ref, at, dot_nt(same, jnp.concatenate([matrix, matrix[MAIN:]], axis=0)))
    for ref in (fore_ref, adj_ref):
        ref[DEPTH - 64 :, :] = jnp.zeros((64, WIDE), BF)


def make_weights(couplings):
    shape = jax.ShapeDtypeStruct((DEPTH, WIDE), BF)
    return call(weights_kernel, (shape, shape), [], "weights", 16, 2 * 10 * DOF * DOF * WIDE)(couplings)


def put_rows(ref, row, source, slot, half):
    for r in range(NRAD):
        ref[row * LINE + r * RADB : row * LINE + (r + 1) * RADB, :] = source[slot + r, half * RADB : (half + 1) * RADB, :]


def spread_bits(field, masks, first, last):
    a, b = first * LINE, last * LINE
    pick = jnp.where(iota((128, 512), 0) == 64 + iota((128, 512), 1) // 128, 1.0, 0.0).astype(BF)
    tail = field[a:b, MAIN:]
    spread = dot(tail, pick)
    place = iota((b - a, 128), 0) % LINE
    masks[a:b, :256] = spread[:, :256].astype(BF)
    masks[a:b, 256:384] = jnp.where(place > 0, spread[:, 256:384], 0.0).astype(BF)
    masks[a:b, 384:] = jnp.where(place < LINE - 1, spread[:, 384:], 0.0).astype(BF)
    tail = tail.astype(F32)
    tail = jnp.where(iota((b - a, 128), 1) < 64, tail, pltpu.roll(tail, 64, 1))
    field[a:b, MAIN:] = tail.astype(BF)


def sides(value, masks, left, right, first, last):
    a, b = first * LINE, last * LINE
    down, up = pltpu.roll(value, 1, 0).astype(BF), pltpu.roll(value, b - a - 1, 0).astype(BF)
    for t in range(3):
        cols = slice(128 * t, 128 * t + 128)
        left[a:b, cols] = down[:, cols] * masks[a:b, 256:384]
        right[a:b, cols] = up[:, cols] * masks[a:b, 384:]


def stencil(field, masks, left, right, weights, first, last):
    a, b = first * LINE, last * LINE
    first_half = iota((b - a, 128), 1) < 64
    m0, m1 = masks[a:b, :128], masks[a:b, 128:256]
    prev, own, nxt = field[a - LINE : b - LINE, :], field[a:b, :], field[a + LINE : b + LINE, :]
    lhs = jnp.concatenate(
        [
            own[:, :MAIN],
            prev[:, :128] * m0,
            prev[:, 128:256] * m0,
            nxt[:, :128] * m1,
            nxt[:, 128:256] * m1,
            left[a:b, :MAIN],
            right[a:b, :MAIN],
            jnp.where(first_half, own[:, MAIN:], prev[:, MAIN:] * m0),
            jnp.where(first_half, nxt[:, MAIN:] * m1, left[a:b, MAIN:]),
            right[a:b, MAIN:],
        ],
        axis=1,
    )
    return dot(lhs, weights[...])


KEEP = []
for level in range(4):
    lo, hi = HALO + level, WINDOW - HALO - 1 - level
    edge = [lo, lo + 1, hi - 1, hi] if level < 3 else [lo, hi]
    KEEP += [(0, level, row) for row in edge]
    KEEP += [(side, level, row) for side in (1, 2) for row in (lo, hi)]
INNER = WINDOW - 2 * HALO


def inner_kernel(mine_ref, fore_ref, adj_ref, keep_ref, mask_ref, s_a, s_b, left, right):
    for i in range(INNER):
        put_rows(s_a, i, mine_ref, (i // AXB) * NRAD, i % AXB)
    spread_bits(s_a, mask_ref, 0, INNER)
    sides(s_a[...].astype(F32), mask_ref, left, right, 0, INNER)

    def keep(level, field):
        for at, (kind, of, row) in enumerate(KEEP):
            if of == level:
                a = (row - HALO) * LINE
                keep_ref[at * LINE : (at + 1) * LINE, :] = (field, left, right)[kind][a : a + LINE, :]

    keep(0, s_a)
    now, later = s_a, s_b
    for level in range(1, 4):
        first, last = level, INNER - level
        value = stencil(now, mask_ref, left, right, fore_ref if level <= STEPS else adj_ref, first, last)
        later[first * LINE : last * LINE, :] = value.astype(BF)
        sides(value, mask_ref, left, right, first, last)
        keep(level, later)
        now, later = later, now


def inner(mine, fore, adj):
    field = pltpu.VMEM((INNER * LINE, WIDE), BF)
    return call(
        inner_kernel,
        (jax.ShapeDtypeStruct((len(KEEP) * LINE, WIDE), BF), jax.ShapeDtypeStruct((INNER * LINE, 512), BF)),
        [field, field, field, field],
        "inner",
        24,
        2 * 12 * LINE * DEPTH * WIDE,
    )(mine, fore, adj)


def outer_kernel(low_ref, high_ref, keep_ref, mask_ref, fore_ref, adj_ref, out_ref, s_a, s_b, left, right, masks):
    for i in range(HALO):
        put_rows(s_a, i, low_ref, (i // AXB) * NRAD, i % AXB)
        put_rows(s_a, WINDOW - HALO + i, high_ref, (i // AXB) * NRAD, i % AXB)
    masks[HALO * LINE : (WINDOW - HALO) * LINE, :] = mask_ref[...]
    for first, last in ((0, HALO), (WINDOW - HALO, WINDOW)):
        spread_bits(s_a, masks, first, last)
        sides(s_a[first * LINE : last * LINE, :].astype(F32), masks, left, right, first, last)

    now, later = s_a, s_b
    for level in range(4):
        for at, (kind, of, row) in enumerate(KEEP):
            if of == level:
                (now, left, right)[kind][row * LINE : (row + 1) * LINE, :] = keep_ref[at * LINE : (at + 1) * LINE, :]
        for first in (level + 1, WINDOW - HALO - 1 - level):
            last = first + HALO
            value = stencil(now, masks, left, right, fore_ref if level < STEPS else adj_ref, first, last)
            later[first * LINE : last * LINE, :] = value.astype(BF)
            if level < 3:
                sides(value, masks, left, right, first, last)
        now, later = later, now

    early = iota((RADB, 128), 1) < 64
    for y in range(RING):
        for r in range(NRAD):
            rows = [(HALO + y * AXB + half) * LINE + r * RADB for half in range(AXB)]
            slot = y * NRAD + r
            for half, row in enumerate(rows):
                out_ref[slot, half * RADB : (half + 1) * RADB, :] = now[row : row + RADB, :128]
                out_ref[slot, BLOCKS + half * RADB : BLOCKS + (half + 1) * RADB, :] = now[row : row + RADB, 128:256]
            out_ref[slot, 2 * BLOCKS :, :] = jnp.where(early, now[rows[0] : rows[0] + RADB, MAIN:], now[rows[1] : rows[1] + RADB, MAIN:])


def outer(low, high, keep, masks, fore, adj):
    field = pltpu.VMEM((WINDOW * LINE, WIDE), BF)
    return call(
        outer_kernel,
        jax.ShapeDtypeStruct((FORC, PACKED, 128), BF),
        [field, field, field, field, pltpu.VMEM((WINDOW * LINE, 512), BF)],
        "outer",
        24,
        2 * 32 * LINE * DEPTH * WIDE,
    )(low, high, keep, masks, fore, adj)


def project_kernel(back_ref, shapes_ref, column_ref, prev_ref, own_ref, next_ref):
    shapes = shapes_ref[...].astype(F32)
    tails = jnp.concatenate([shapes[:RADB, MAIN:], shapes[RADB:, MAIN:]], axis=1)
    back = back_ref[...].astype(F32)
    body_sum = back[:, :BLOCKS] * shapes[None, :, :128] + back[:, BLOCKS : 2 * BLOCKS] * shapes[None, :, 128:256]
    tail = back[:, 2 * BLOCKS :] * tails[None]
    early = iota((FORC, RADB, 128), 2) < 64
    tail = jnp.concatenate([jnp.where(early, tail, 0.0), jnp.where(early, 0.0, tail)], axis=1)
    proj = jnp.sum(body_sum + tail, axis=2, keepdims=True)
    lane = iota((BLOCKS, 128), 1)
    by_block = jnp.zeros((BLOCKS, 128), F32)
    for f in range(FORC):
        by_block = jnp.where(lane == f, proj[f], by_block)
    column = column_ref[...]
    for at, ref in enumerate((prev_ref, own_ref, next_ref)):
        for slot in range(4):
            part = jnp.sum(jnp.where(column == 4 * at + slot, by_block, 0.0), axis=0, keepdims=True)
            ref[slot : slot + 1, :] = part[:, :FORC]


def project(back, shapes, column):
    part = jax.ShapeDtypeStruct((4, FORC), F32)
    return call(project_kernel, (part, part, part), [], "project", 16, 2 * ROWS * DOF)(back, shapes, column)


def place_kernel(back_ref, state_ref, wide):
    for f in range(FORC):
        row = f * BLOCKS
        wide[row : row + BLOCKS, :128] = back_ref[f, :BLOCKS, :]
        wide[row : row + BLOCKS, 128:256] = back_ref[f, BLOCKS : 2 * BLOCKS, :]
        tail = back_ref[f, 2 * BLOCKS :, :]
        wide[row : row + RADB, MAIN:] = tail
        wide[row + RADB : row + BLOCKS, MAIN:] = pltpu.roll(tail.astype(F32), 64, 1).astype(BF)
    order = one_hot(ROWS, ROWS, lambda o: (o % FORC) * BLOCKS + o // FORC)
    state_ref[...] = dot(order, wide[...])[:, :DOF].astype(BF)


def place(back):
    return call(
        place_kernel, jax.ShapeDtypeStruct((ROWS, DOF), BF), [pltpu.VMEM((ROWS, WIDE), BF)], "place", 16, 2 * ROWS * ROWS * WIDE
    )(back)


def body(state, bits, couplings, shapes, amap):
    n_h, n_rad = lax.axis_size("h"), lax.axis_size("r")
    h, y, r = lax.axis_index("h"), lax.axis_index("y"), lax.axis_index("r")
    per_group = ACT // (n_h * RING * n_rad)
    ahead = [(i, i + 1) for i in range(n_h - 1)]
    back = [(b, a) for a, b in ahead]

    send = pack(state.reshape(ROWS, DOF), bits.transpose(0, 2, 1))
    mine = lax.all_to_all(send, ("y", "r"), 0, 0, tiled=True)
    fore, adj = make_weights(couplings)
    reach = HALO // AXB * n_rad
    low = lax.ppermute(mine[-reach:], "h", ahead)
    high = lax.ppermute(mine[:reach], "h", back)
    keep, masks = inner(mine, fore, adj)
    out = outer(low, high, keep, masks, fore, adj)
    back_home = lax.all_to_all(out, ("y", "r"), 0, 0, tiled=True)

    amap = amap.reshape(BLOCKS, 1)
    shift = (amap // per_group - ((h * RING + y) * n_rad + r)) // n_rad
    column = (shift + 1) * per_group + amap % per_group
    to_prev, own, to_next = project(back_home, shapes.reshape(BLOCKS, DOF), column)
    n_ax = n_h * RING
    up = [(i, i + 1) for i in range(n_ax - 1)]
    from_prev = lax.ppermute(to_next, ("h", "y"), up)
    from_next = lax.ppermute(to_prev, ("h", "y"), [(b, a) for a, b in up])
    result = place(back_home)
    return result.reshape(state.shape), (own + from_prev + from_next).T


def solution(mesh):
    n_ax, n_rad = mesh.shape["ax"], mesh.shape["rad"]
    fine = Mesh(mesh.devices.reshape(n_ax // RING, RING, n_rad), ("h", "y", "r"))
    ax = ("h", "y")
    in_specs = (P(ax, "r"), P(ax, "r"), P(), P(ax, "r"), P(ax, "r"))
    out_specs = (P(ax, "r"), P(None, ("h", "y", "r")))
    return jax.shard_map(body, mesh=fine, in_specs=in_specs, out_specs=out_specs, check_vma=False)
```

time: 91.1 us -> 77.9 us (0.86)
  local copies, waits for them, and re-layouts: 21.8 us -> 1.81 us
  blocking collectives: 0 us -> 19 us
  starting transfers between devices: 28.9 us -> 20.7 us
  waiting for transfers between devices: 25.6 us -> 21.9 us
  Pallas kernels: 9.6 us -> 11.9 us
  other arithmetic: 2.64 us -> 0.63 us
    all_to_all x0 -> x1, blocking collectives: none -> 19 us  [body(): mine = lax.all_to_all(send, ('y', 'r'), 0, 0, tiled=True)]
    unnamed x36 -> x10, local copies, waits for them, and re-layouts: 18.8 us -> 1.69 us
    all_to_all x1 -> x0, starting transfers between devices: 7.65 us -> none  [body(): mine = lax.all_to_all(send, ('y', 'r'), 0, 0, tiled=True)]
    pallas_call x3 -> x6, Pallas kernels: 9.6 us -> 11.9 us  [the longest x1 5.4 us: outer(): call(outer_kernel, jax.ShapeDtypeStruct((FORC, PACKED, 128), BF), [field,...]
    ppermute x1, waiting for transfers between devices: 7.12 us -> 5 us  [body(): high = lax.ppermute(mine[:reach], 'h', back)]
    slice x3 -> x0, local copies, waits for them, and re-layouts: 2.08 us -> none  [the longest x2 1.06 us: stacked(): return jnp.concatenate([rows, rows[:, MAIN:]], axis=1)]
    concatenate x1 -> x0, other arithmetic: 1.84 us -> none  [stacked(): return jnp.concatenate([rows, rows[:, MAIN:]], axis=1)]
    ppermute x1, waiting for transfers between devices: 8.47 us -> 7.15 us  [body(): from_next = lax.ppermute(to_prev, ('h', 'y'), [(b, a) for a, b in up])]
  transfers between devices with their start and end apart: 6 -> 5, of which waited for: 4 -> 3; matrix products, arithmetic and copies ran while one was open for 24% -> 0% of each run, Pallas kernels for 0% -> 7%
where the time goes in v3:
time: 77.9 us; the launch traced here: 76.7 us
  waiting for transfers between devices  21.9 us (28%)
  starting transfers between devices  20.7 us (27%)
  blocking collectives  19 us (24%)
  Pallas kernels  11.9 us (15%)
  local copies, waits for them, and re-layouts  1.81 us (2%)
    all_to_all x1, blocking collectives, body(): mine = lax.all_to_all(send, ('y', 'r'), 0, 0, tiled=True)  19 us
    all_to_all x1, waiting for transfers between devices, body(): back_home = lax.all_to_all(out, ('y', 'r'), 0, 0, tiled=True)  9.74 us
    all_to_all x1, starting transfers between devices, body(): back_home = lax.all_to_all(out, ('y', 'r'), 0, 0, tiled=True)  7.82 us
    ppermute x1, waiting for transfers between devices, body(): from_next = lax.ppermute(to_prev, ('h', 'y'), [(b, a) for a, b in up])  7.15 us
    pallas_call x1, Pallas kernels, outer(): call(outer_kernel, jax.ShapeDtypeStruct((FORC, PACKED, 128), BF), [field,...  5.4 us
    ppermute x1, starting transfers between devices, body(): low = lax.ppermute(mine[-reach:], 'h', ahead)  5.13 us
    ppermute x1, waiting for transfers between devices, body(): high = lax.ppermute(mine[:reach], 'h', back)  5 us
    ppermute x1, starting transfers between devices, body(): from_prev = lax.ppermute(to_next, ('h', 'y'), up)  3.93 us
  transfers between devices with their start and end apart: 5, of which 3 were waited for; matrix products, arithmetic and copies ran while one was open for 0% of the time, Pallas kernels for 7%

profile of v3, /device:TPU:479, one launch (start us, length us, event | category | flops | bytes accessed | tf_op | source)
XLA Modules:
  0.0 76.7 jit_solution(13068284097024864590)
XLA Ops:
  0.6 0.0 copy-start
  0.6 1.0 %copy-done = bf16[2,16,16,320]{3,2,1,0:T(8,128)(2,1)S(1)} copy-done((bf16[2,16,16,320]{3,2,1,0:T(8,128)(2,1)S(1)}, bf16[2,16,16,320]{3,2,1,0:T(8,128)(2,1)}, u32[]{:S(2)}) %copy-start) | copy-done | bytes 327704
  1.6 0.7 copy-done.2
  2.3 1.0 %pack.1 = bf16[16,32,384]{2,1,0:T(8,128)(2,1)S(1)} custom-call(bf16[512,320]{1,0:T(8,128)(2,1)S(1)} %bitcast.6, s32[2,4,16]{2,1,0:T(4,128)S(1)} %bitcast.8), custom_call_target="tpu_custom_call" | custom-call | flops 201326592 | bytes 2097152 | tf_op jit(solution)/shard_map/pack/pallas_call | solution.py:75
  3.3 19.0 %all_to_all.10.mine_ref = bf16[16,32,384]{2,1,0:T(8,128)(2,1)S(1)} all-to-all(bf16[16,32,384]{2,1,0:T(8,128)(2,1)S(1)} %pack.1), channel_id=1, replica_groups=mesh['h'=64,'y'=4,'r'=4] {'y','r'}, dimensions={0} | all-to-all | bytes 786432 | tf_op jit(solution)/shard_map/all_to_all | solution.py:304
  22.3 5.1 %collective-permute-start = (bf16[8,32,384]{2,1,0:T(8,128)(2,1)S(1)}, bf16[8,32,384]{2,1,0:T(8,128)(2,1)S(1)}, u32[]{:S(2)}, u32[]{:S(2)}) collective-permute-start(bf16[8,32,384]{2,1,0:T(8,128)(2,1)S(1)} %get-tuple-element.17), channel_id=1, source_target_pairs={{0,16},{16,32},{32,48},{48,64},{64,80},{80,96},{96,112},{112,128},... | collective-permute-start | bytes 589832 | tf_op jit(solution)/shard_map/ppermute | solution.py:307
  27.5 1.9 %collective-permute-start.1 = (bf16[8,32,384]{2,1,0:T(8,128)(2,1)S(1)}, bf16[8,32,384]{2,1,0:T(8,128)(2,1)S(1)}, u32[]{:S(2)}, u32[]{:S(2)}) collective-permute-start(bf16[8,32,384]{2,1,0:T(8,128)(2,1)S(1)} %get-tuple-element.16), channel_id=1, source_target_pairs={{16,0},{32,16},{48,32},{64,48},{80,64},{96,80},{112,96},{128,112},... | collective-permute-start | bytes 589832 | tf_op jit(solution)/shard_map/ppermute | solution.py:308
  29.4 0.0 copy-done.3
  29.4 1.6 %weights.1 = (bf16[1664,384]{1,0:T(8,128)(2,1)S(1)}, bf16[1664,384]{1,0:T(8,128)(2,1)S(1)}) custom-call(bf16[5,320,320]{2,1,0:T(8,128)(2,1)S(1)} %copy-done.3), custom_call_target="tpu_custom_call" | custom-call | flops 786432000 | bytes 2097152 | tf_op jit(solution)/shard_map/weights/pallas_call | solution.py:110
  31.0 2.4 %inner.1 = (bf16[1920,384]{1,0:T(8,128)(2,1)S(1)}, bf16[512,512]{1,0:T(8,128)(2,1)S(1)}) custom-call(bf16[16,32,384]{2,1,0:T(8,128)(2,1)S(1)} %all_to_all.10.mine_ref, bf16[1664,384]{1,0:T(8,128)(2,1)S(1)} %get-tuple-element.9.fore_ref, bf16[1664,384]{1,0:T(8,128)(2,1)S(1)} %get-tuple-element.10.adj_ref), custom_call_target="tpu_custom_call" | custom-call | flops 981467136 | bytes 2097152 | tf_op jit(solution)/shard_map/inner/pallas_call | solution.py:198
  33.4 0.0 collective-permute-done.low_ref
  33.4 5.0 %collective-permute-done.1.high_ref = bf16[8,32,384]{2,1,0:T(8,128)(2,1)S(1)} collective-permute-done((bf16[8,32,384]{2,1,0:T(8,128)(2,1)S(1)}, bf16[8,32,384]{2,1,0:T(8,128)(2,1)S(1)}, u32[]{:S(2)}, u32[]{:S(2)}) %collective-permute-start.1) | collective-permute-done | bytes 196640 | tf_op jit(solution)/shard_map/ppermute | solution.py:308
  38.4 5.4 %outer.1 = bf16[16,80,128]{2,1,0:T(8,128)(2,1)} custom-call(bf16[8,32,384]{2,1,0:T(8,128)(2,1)S(1)} %collective-permute-done.low_ref, bf16[8,32,384]{2,1,0:T(8,128)(2,1)S(1)} %collective-permute-done.1.high_ref, bf16[1920,384]{1,0:T(8,128)(2,1)S(1)} %get-tuple-element.11.keep_ref, bf16[512,512]{1,0:T(8,128)(2,1)S(1)} %get-tuple-element.12.mask_ref, ...), custom_call_target="tpu_custom_call" | custom-call | flops 2617245696 | bytes 2097152 | tf_op jit(solution)/shard_map/outer/pallas_call | solution.py:243
  43.8 7.8 %all-to-all-start.1 = ((bf16[16,80,128]{2,1,0:T(8,128)(2,1)}), bf16[16,80,128]{2,1,0:T(8,128)(2,1)S(1)}, u32[]{:S(2)}, u32[]{:S(2)}) async-start(bf16[16,80,128]{2,1,0:T(8,128)(2,1)} %outer.1), calls=%async_computation.1 | async-start | bytes 655360 | tf_op jit(solution)/shard_map/all_to_all | solution.py:311
  51.6 0.0 copy-done.4
  51.6 0.1 reshape.233
  51.8 9.7 %all-to-all-done.1.back_ref = bf16[16,80,128]{2,1,0:T(8,128)(2,1)S(1)} async-done(((bf16[16,80,128]{2,1,0:T(8,128)(2,1)}), bf16[16,80,128]{2,1,0:T(8,128)(2,1)S(1)}, u32[]{:S(2)}, u32[]{:S(2)}) %all-to-all-start.1) | async-done | bytes 327712 | tf_op jit(solution)/shard_map/all_to_all | solution.py:311
  61.5 0.3 project.1
  61.8 3.9 %collective-permute-start.2 = (f32[4,16]{1,0:T(4,128)S(1)}, f32[4,16]{1,0:T(4,128)S(1)}, u32[]{:S(2)}, u32[]{:S(2)}) collective-permute-start(f32[4,16]{1,0:T(4,128)S(1)} %get-tuple-element.14), channel_id=1, source_target_pairs={{0,4},{4,8},{8,12},{12,16},{16,20},{20,24},{24,28},{28,32},{32,36}... | collective-permute-start | bytes 776 | tf_op jit(solution)/shard_map/ppermute | solution.py:319
  65.8 1.9 %collective-permute-start.3 = (f32[4,16]{1,0:T(4,128)S(1)}, f32[4,16]{1,0:T(4,128)S(1)}, u32[]{:S(2)}, u32[]{:S(2)}) collective-permute-start(f32[4,16]{1,0:T(4,128)S(1)} %get-tuple-element.15), channel_id=1, source_target_pairs={{4,0},{8,4},{12,8},{16,12},{20,16},{24,20},{28,24},{32,28},{36,32}... | collective-permute-start | bytes 776 | tf_op jit(solution)/shard_map/ppermute | solution.py:320
  67.7 1.3 %place.1 = bf16[512,320]{1,0:T(8,128)(2,1)} custom-call(bf16[16,80,128]{2,1,0:T(8,128)(2,1)S(1)} %all-to-all-done.1.back_ref), custom_call_target="tpu_custom_call" | custom-call | flops 201326592 | bytes 2097152 | tf_op jit(solution)/shard_map/place/pallas_call | solution.py:291
  69.0 0.0 collective-permute-done.2
  69.0 7.1 %collective-permute-done.3 = f32[4,16]{1,0:T(4,128)S(1)} collective-permute-done((f32[4,16]{1,0:T(4,128)S(1)}, f32[4,16]{1,0:T(4,128)S(1)}, u32[]{:S(2)}, u32[]{:S(2)}) %collective-permute-start.3) | collective-permute-done | bytes 288 | tf_op jit(solution)/shard_map/ppermute | solution.py:320
  76.1 0.6 add_bitcast_fusion
  (7 shorter events, 0.1 us)
Async XLA Ops:
  0.6 1.0 %copy-start = (bf16[2,16,16,320]{3,2,1,0:T(8,128)(2,1)S(1)}, bf16[2,16,16,320]{3,2,1,0:T(8,128)(2,1)}, u32[]{:S(2)}) copy-start(bf16[2,16,16,320]{3,2,1,0:T(8,128)(2,1)} %param.5) | copy-start | bytes 983044
  1.6 0.7 copy-start.2
  2.3 27.1 %copy-start.3 = (bf16[5,320,320]{2,1,0:T(8,128)(2,1)S(1)}, bf16[5,320,320]{2,1,0:T(8,128)(2,1)}, u32[]{:S(2)}) copy-start(bf16[5,320,320]{2,1,0:T(8,128)(2,1)} %couplings_ref.1) | copy-start | bytes 3072004
  22.3 11.1 %collective-permute-start = (bf16[8,32,384]{2,1,0:T(8,128)(2,1)S(1)}, bf16[8,32,384]{2,1,0:T(8,128)(2,1)S(1)}, u32[]{:S(2)}, u32[]{:S(2)}) collective-permute-start(bf16[8,32,384]{2,1,0:T(8,128)(2,1)S(1)} %get-tuple-element.17), channel_id=1, source_target_pairs={{0,16},{16,32},{32,48},{48,64},{64,80},{80,96},{96,112},{112,128},... | collective-permute-start | bytes 589832 | tf_op jit(solution)/shard_map/ppermute | solution.py:307
  27.5 10.9 %collective-permute-start.1 = (bf16[8,32,384]{2,1,0:T(8,128)(2,1)S(1)}, bf16[8,32,384]{2,1,0:T(8,128)(2,1)S(1)}, u32[]{:S(2)}, u32[]{:S(2)}) collective-permute-start(bf16[8,32,384]{2,1,0:T(8,128)(2,1)S(1)} %get-tuple-element.16), channel_id=1, source_target_pairs={{16,0},{32,16},{48,32},{64,48},{80,64},{96,80},{112,96},{128,112},... | collective-permute-start | bytes 589832 | tf_op jit(solution)/shard_map/ppermute | solution.py:308
  38.4 13.2 %copy-start.4 = (s32[2,16]{1,0:T(2,128)S(1)}, s32[2,16]{1,0:T(2,128)}, u32[]{:S(2)}) copy-start(s32[2,16]{1,0:T(2,128)} %param.9) | copy-start | bytes 388
  38.4 23.1 %copy-start.1 = (bf16[2,16,320]{2,1,0:T(8,128)(2,1)S(1)}, bf16[2,16,320]{2,1,0:T(8,128)(2,1)}, u32[]{:S(2)}) copy-start(bf16[2,16,320]{2,1,0:T(8,128)(2,1)} %param.8) | copy-start | bytes 61444
  43.8 17.7 %all-to-all-start.1 = ((bf16[16,80,128]{2,1,0:T(8,128)(2,1)}), bf16[16,80,128]{2,1,0:T(8,128)(2,1)S(1)}, u32[]{:S(2)}, u32[]{:S(2)}) async-start(bf16[16,80,128]{2,1,0:T(8,128)(2,1)} %outer.1), calls=%async_computation.1 | async-start | bytes 655360 | tf_op jit(solution)/shard_map/all_to_all | solution.py:311
  61.8 7.1 %collective-permute-start.2 = (f32[4,16]{1,0:T(4,128)S(1)}, f32[4,16]{1,0:T(4,128)S(1)}, u32[]{:S(2)}, u32[]{:S(2)}) collective-permute-start(f32[4,16]{1,0:T(4,128)S(1)} %get-tuple-element.14), channel_id=1, source_target_pairs={{0,4},{4,8},{8,12},{12,16},{16,20},{20,24},{24,28},{28,32},{32,36}... | collective-permute-start | bytes 776 | tf_op jit(solution)/shard_map/ppermute | solution.py:319
  65.8 10.3 %collective-permute-start.3 = (f32[4,16]{1,0:T(4,128)S(1)}, f32[4,16]{1,0:T(4,128)S(1)}, u32[]{:S(2)}, u32[]{:S(2)}) collective-permute-start(f32[4,16]{1,0:T(4,128)S(1)} %get-tuple-element.15), channel_id=1, source_target_pairs={{4,0},{8,4},{12,8},{16,12},{20,16},{24,20},{28,24},{32,28},{36,32}... | collective-permute-start | bytes 776 | tf_op jit(solution)/shard_map/ppermute | solution.py:320

commit v4 on v3

--- a/solution.py
+++ b/solution.py
@@ -1,3 +1,5 @@
+import functools
+
 import jax
 import jax.numpy as jnp
 from jax import lax
@@ -54,15 +56,18 @@
     )
 
 
-def pack_kernel(state_ref, bits_ref, out_ref, rows, wide, bits, sem):
-    copy = pltpu.make_async_copy(state_ref, rows, sem)
+def pack_kernel(state_ref, bits_ref, out_ref, rows, links, wide, bits, sems):
+    copy = pltpu.make_async_copy(state_ref, rows, sems.at[0])
+    link_copy = pltpu.make_async_copy(bits_ref, links, sems.at[1])
+    link_copy.start()
     copy.start()
     order = one_hot(ROWS, ROWS, lambda o: (o % BLOCKS) * FORC + o // BLOCKS)
     bits[...] = jnp.zeros_like(bits)
+    wide[:, MAIN:] = jnp.zeros((ROWS, 128), BF)
+    link_copy.wait()
     for a in range(AXB):
-        bits[a, 64:68, :RADB] = bits_ref[a].astype(F32)
+        bits[a, 64:68, :RADB] = links[a].astype(F32)
     spread = [dot_nt(one_hot(ROWS, 128, lambda o: o % BLOCKS - a * RADB), bits[a].astype(BF)) for a in range(AXB)]
-    wide[:, MAIN:] = jnp.zeros((ROWS, 128), BF)
     copy.wait()
     wide[:, :DOF] = rows[...]
     out = dot(order, wide[...]).astype(BF)
@@ -75,15 +80,21 @@
     return call(
         pack_kernel,
         jax.ShapeDtypeStruct((FORC, BLOCKS, WIDE), BF),
-        [pltpu.VMEM((ROWS, DOF), BF), pltpu.VMEM((ROWS, WIDE), BF), pltpu.VMEM((AXB, 128, 128), F32), pltpu.SemaphoreType.DMA],
+        [
+            pltpu.VMEM((ROWS, DOF), BF),
+            pltpu.VMEM((AXB, 4, RADB), jnp.int32),
+            pltpu.VMEM((ROWS, WIDE), BF),
+            pltpu.VMEM((AXB, 128, 128), F32),
+            pltpu.SemaphoreType.DMA((2,)),
+        ],
         "pack",
         16,
         2 * ROWS * ROWS * WIDE,
-        [pl.BlockSpec(memory_space=pl.ANY), pl.BlockSpec(memory_space=pltpu.VMEM)],
+        [pl.BlockSpec(memory_space=pltpu.HBM)] * 2,
     )(state, bits)
 
 
-def weights_kernel(couplings_ref, fore_ref, adj_ref):
+def stack_weights(couplings_ref, fore_ref, adj_ref):
     twice = jnp.where(
         (iota((DOF, WIDE), 1) == iota((DOF, WIDE), 0)) | (iota((DOF, WIDE), 1) == iota((DOF, WIDE), 0) + 64)
         & (iota((DOF, WIDE), 1) >= DOF),
@@ -103,11 +114,6 @@
         put(adj_ref, at, dot_nt(same, jnp.concatenate([matrix, matrix[MAIN:]], axis=0)))
     for ref in (fore_ref, adj_ref):
         ref[DEPTH - 64 :, :] = jnp.zeros((64, WIDE), BF)
-
-
-def make_weights(couplings):
-    shape = jax.ShapeDtypeStruct((DEPTH, WIDE), BF)
-    return call(weights_kernel, (shape, shape), [], "weights", 16, 2 * 10 * DOF * DOF * WIDE)(couplings)
 
 
 def put_rows(ref, row, source, slot, half):
@@ -170,7 +176,8 @@
 INNER = WINDOW - 2 * HALO
 
 
-def inner_kernel(mine_ref, fore_ref, adj_ref, keep_ref, mask_ref, s_a, s_b, left, right):
+def inner_kernel(mine_ref, couplings_ref, fore_ref, adj_ref, keep_ref, mask_ref, s_a, s_b, left, right):
+    stack_weights(couplings_ref, fore_ref, adj_ref)
     for i in range(INNER):
         put_rows(s_a, i, mine_ref, (i // AXB) * NRAD, i % AXB)
     spread_bits(s_a, mask_ref, 0, INNER)
@@ -193,61 +200,68 @@
         now, later = later, now
 
 
-def inner(mine, fore, adj):
+def inner(mine, couplings):
     field = pltpu.VMEM((INNER * LINE, WIDE), BF)
+    weights = jax.ShapeDtypeStruct((DEPTH, WIDE), BF)
     return call(
         inner_kernel,
-        (jax.ShapeDtypeStruct((len(KEEP) * LINE, WIDE), BF), jax.ShapeDtypeStruct((INNER * LINE, 512), BF)),
+        (weights, weights, jax.ShapeDtypeStruct((len(KEEP) * LINE, WIDE), BF), jax.ShapeDtypeStruct((INNER * LINE, 512), BF)),
         [field, field, field, field],
         "inner",
         24,
         2 * 12 * LINE * DEPTH * WIDE,
-    )(mine, fore, adj)
-
-
-def outer_kernel(low_ref, high_ref, keep_ref, mask_ref, fore_ref, adj_ref, out_ref, s_a, s_b, left, right, masks):
+    )(mine, couplings)
+
+
+def outer_kernel(upper, *refs):
+    halo_ref, keep_ref, mask_ref, fore_ref, adj_ref = refs[:5]
+    out_ref, s_a, s_b, left, right, masks = refs[-6:]
+    edge = WINDOW - HALO if upper else 0
     for i in range(HALO):
-        put_rows(s_a, i, low_ref, (i // AXB) * NRAD, i % AXB)
-        put_rows(s_a, WINDOW - HALO + i, high_ref, (i // AXB) * NRAD, i % AXB)
-    masks[HALO * LINE : (WINDOW - HALO) * LINE, :] = mask_ref[...]
-    for first, last in ((0, HALO), (WINDOW - HALO, WINDOW)):
-        spread_bits(s_a, masks, first, last)
-        sides(s_a[first * LINE : last * LINE, :].astype(F32), masks, left, right, first, last)
+        put_rows(s_a, edge + i, halo_ref, (i // AXB) * NRAD, i % AXB)
+    half = WINDOW // 2 if upper else HALO
+    at = (half - HALO) * LINE
+    masks[half * LINE : (half + HALO) * LINE, :] = mask_ref[at : at + HALO * LINE, :]
+    spread_bits(s_a, masks, edge, edge + HALO)
+    sides(s_a[edge * LINE : (edge + HALO) * LINE, :].astype(F32), masks, left, right, edge, edge + HALO)
 
     now, later = s_a, s_b
     for level in range(4):
         for at, (kind, of, row) in enumerate(KEEP):
             if of == level:
                 (now, left, right)[kind][row * LINE : (row + 1) * LINE, :] = keep_ref[at * LINE : (at + 1) * LINE, :]
-        for first in (level + 1, WINDOW - HALO - 1 - level):
-            last = first + HALO
-            value = stencil(now, masks, left, right, fore_ref if level < STEPS else adj_ref, first, last)
-            later[first * LINE : last * LINE, :] = value.astype(BF)
-            if level < 3:
-                sides(value, masks, left, right, first, last)
+        first = WINDOW - HALO - 1 - level if upper else level + 1
+        last = first + HALO
+        value = stencil(now, masks, left, right, fore_ref if level < STEPS else adj_ref, first, last)
+        later[first * LINE : last * LINE, :] = value.astype(BF)
+        if level < 3:
+            sides(value, masks, left, right, first, last)
         now, later = later, now
 
     early = iota((RADB, 128), 1) < 64
-    for y in range(RING):
-        for r in range(NRAD):
-            rows = [(HALO + y * AXB + half) * LINE + r * RADB for half in range(AXB)]
-            slot = y * NRAD + r
-            for half, row in enumerate(rows):
-                out_ref[slot, half * RADB : (half + 1) * RADB, :] = now[row : row + RADB, :128]
-                out_ref[slot, BLOCKS + half * RADB : BLOCKS + (half + 1) * RADB, :] = now[row : row + RADB, 128:256]
-            out_ref[slot, 2 * BLOCKS :, :] = jnp.where(early, now[rows[0] : rows[0] + RADB, MAIN:], now[rows[1] : rows[1] + RADB, MAIN:])
-
-
-def outer(low, high, keep, masks, fore, adj):
+    slots = FORC // 2
+    if upper:
+        out_ref[:slots] = refs[5][...]
+    for slot in range(slots):
+        y, r = slot // NRAD, slot % NRAD
+        rows = [(half + y * AXB + a) * LINE + r * RADB for a in range(AXB)]
+        to = slot + (slots if upper else 0)
+        for a, row in enumerate(rows):
+            out_ref[to, a * RADB : (a + 1) * RADB, :] = now[row : row + RADB, :128]
+            out_ref[to, BLOCKS + a * RADB : BLOCKS + (a + 1) * RADB, :] = now[row : row + RADB, 128:256]
+        out_ref[to, 2 * BLOCKS :, :] = jnp.where(early, now[rows[0] : rows[0] + RADB, MAIN:], now[rows[1] : rows[1] + RADB, MAIN:])
+
+
+def outer(upper, *args):
     field = pltpu.VMEM((WINDOW * LINE, WIDE), BF)
     return call(
-        outer_kernel,
-        jax.ShapeDtypeStruct((FORC, PACKED, 128), BF),
+        functools.partial(outer_kernel, upper),
+        jax.ShapeDtypeStruct((FORC if upper else FORC // 2, PACKED, 128), BF),
         [field, field, field, field, pltpu.VMEM((WINDOW * LINE, 512), BF)],
-        "outer",
+        "upper" if upper else "lower",
         24,
-        2 * 32 * LINE * DEPTH * WIDE,
-    )(low, high, keep, masks, fore, adj)
+        2 * 16 * LINE * DEPTH * WIDE,
+    )(*args)
 
 
 def project_kernel(back_ref, shapes_ref, column_ref, prev_ref, own_ref, next_ref):
@@ -293,6 +307,10 @@
     )(back)
 
 
+def swaps(firsts):
+    return [pair for i in firsts for pair in ((i, i + 1), (i + 1, i))]
+
+
 def body(state, bits, couplings, shapes, amap):
     n_h, n_rad = lax.axis_size("h"), lax.axis_size("r")
     h, y, r = lax.axis_index("h"), lax.axis_index("y"), lax.axis_index("r")
@@ -302,24 +320,27 @@
 
     send = pack(state.reshape(ROWS, DOF), bits.transpose(0, 2, 1))
     mine = lax.all_to_all(send, ("y", "r"), 0, 0, tiled=True)
-    fore, adj = make_weights(couplings)
     reach = HALO // AXB * n_rad
     low = lax.ppermute(mine[-reach:], "h", ahead)
     high = lax.ppermute(mine[:reach], "h", back)
-    keep, masks = inner(mine, fore, adj)
-    out = outer(low, high, keep, masks, fore, adj)
-    back_home = lax.all_to_all(out, ("y", "r"), 0, 0, tiled=True)
-
     amap = amap.reshape(BLOCKS, 1)
     shift = (amap // per_group - ((h * RING + y) * n_rad + r)) // n_rad
     column = (shift + 1) * per_group + amap % per_group
+    mine, column = lax.optimization_barrier((mine, column))
+    fore, adj, keep, masks = inner(mine, couplings)
+    lower = outer(False, low, keep, masks, fore, adj)
+    out = outer(True, high, keep, masks, fore, adj, lower)
+    back_home = lax.all_to_all(out, ("y", "r"), 0, 0, tiled=True)
+
     to_prev, own, to_next = project(back_home, shapes.reshape(BLOCKS, DOF), column)
     n_ax = n_h * RING
-    up = [(i, i + 1) for i in range(n_ax - 1)]
-    from_prev = lax.ppermute(to_next, ("h", "y"), up)
-    from_next = lax.ppermute(to_prev, ("h", "y"), [(b, a) for a, b in up])
+    far = swaps(range(1, n_ax - 1, 2))
+    near = swaps(range(0, n_ax - 1, 2))
+    odd = y % 2 == 1
+    from_far = lax.ppermute(jnp.where(odd, to_next, to_prev), ("h", "y"), far)
+    from_near = lax.ppermute(jnp.where(odd, to_prev, to_next), ("h", "y"), near)
     result = place(back_home)
-    return result.reshape(state.shape), (own + from_prev + from_next).T
+    return result.reshape(state.shape), (own + from_far + from_near).T
 
 
 def solution(mesh):

time: 77.9 us -> 74.7 us (0.959)
  the two profiles are of different devices: /device:TPU:479 before, /device:TPU:2 now
where the time goes in v4:
time: 74.7 us; the launch traced here: 74.3 us
  starting transfers between devices  29.5 us (39%)
  waiting for transfers between devices  28.1 us (38%)
  Pallas kernels  13.5 us (18%)
  local copies, waits for them, and re-layouts  1.81 us (2%)
  between operations  0.8 us (1%)
    all_to_all x1, waiting for transfers between devices, body(): mine = lax.all_to_all(send, ('y', 'r'), 0, 0, tiled=True)  14.1 us
    all_to_all x1, waiting for transfers between devices, body(): back_home = lax.all_to_all(out, ('y', 'r'), 0, 0, tiled=True)  12.7 us
    ppermute x1, starting transfers between devices, body(): high = lax.ppermute(mine[:reach], 'h', back)  9.2 us
    all_to_all x1, starting transfers between devices, body(): mine = lax.all_to_all(send, ('y', 'r'), 0, 0, tiled=True)  7.22 us
    pallas_call x2, Pallas kernels, outer(): call(functools.partial(outer_kernel, upper), jax.ShapeDtypeStruct((FORC i...  6.26 us
    pallas_call x1, Pallas kernels, inner(): call(inner_kernel, (weights, weights, jax.ShapeDtypeStruct((len(KEEP) * L...  3.77 us
    all_to_all x1, starting transfers between devices, body(): back_home = lax.all_to_all(out, ('y', 'r'), 0, 0, tiled=True)  3.54 us
    ppermute x1, starting transfers between devices, body(): low = lax.ppermute(mine[-reach:], 'h', ahead)  3.39 us
  transfers between devices with their start and end apart: 6, of which 4 were waited for; matrix products, arithmetic and copies ran while one was open for 0% of the time, Pallas kernels for 11%

profile of v4, /device:TPU:2, one launch (start us, length us, event | category | flops | bytes accessed | tf_op | source)
XLA Modules:
  0.0 74.3 jit_solution(14803294057050906506)
XLA Ops:
  0.7 1.0 %copy-done = bf16[2,16,16,320]{3,2,1,0:T(8,128)(2,1)S(1)} copy-done((bf16[2,16,16,320]{3,2,1,0:T(8,128)(2,1)S(1)}, bf16[2,16,16,320]{3,2,1,0:T(8,128)(2,1)}, u32[]{:S(2)}) %copy-start) | copy-done | bytes 327704
  1.6 0.7 copy-done.2
  2.3 1.9 %pack.1 = bf16[16,32,384]{2,1,0:T(8,128)(2,1)} custom-call(bf16[512,320]{1,0:T(8,128)(2,1)S(1)} %bitcast.6, s32[2,4,16]{2,1,0:T(4,128)S(1)} %bitcast.8), custom_call_target="tpu_custom_call" | custom-call | flops 201326592 | bytes 2097152 | tf_op jit(solution)/shard_map/pack/pallas_call | solution.py:80
  4.2 7.2 %all-to-all-start = ((bf16[16,32,384]{2,1,0:T(8,128)(2,1)}), bf16[16,32,384]{2,1,0:T(8,128)(2,1)S(1)}, u32[]{:S(2)}, u32[]{:S(2)}) async-start(bf16[16,32,384]{2,1,0:T(8,128)(2,1)} %pack.1), calls=%async_computation | async-start | bytes 786432 | tf_op jit(solution)/shard_map/all_to_all | solution.py:322
  11.4 0.1 reshape.233
  11.5 14.1 %all-to-all-done.mine_ref = bf16[16,32,384]{2,1,0:T(8,128)(2,1)S(1)} async-done(((bf16[16,32,384]{2,1,0:T(8,128)(2,1)}), bf16[16,32,384]{2,1,0:T(8,128)(2,1)S(1)}, u32[]{:S(2)}, u32[]{:S(2)}) %all-to-all-start) | async-done | bytes 393248 | tf_op jit(solution)/shard_map/all_to_all | solution.py:322
  25.7 3.4 %collective-permute-start.1 = (bf16[8,32,384]{2,1,0:T(8,128)(2,1)S(1)}, bf16[8,32,384]{2,1,0:T(8,128)(2,1)S(1)}, u32[]{:S(2)}, u32[]{:S(2)}) collective-permute-start(bf16[8,32,384]{2,1,0:T(8,128)(2,1)S(1)} %get-tuple-element.20), channel_id=1, source_target_pairs={{0,16},{16,32},{32,48},{48,64},{64,80},{80,96},{96,112},{112,128},... | collective-permute-start | bytes 589832 | tf_op jit(solution)/shard_map/ppermute | solution.py:324
  29.1 9.2 %collective-permute-start = (bf16[8,32,384]{2,1,0:T(8,128)(2,1)S(1)}, bf16[8,32,384]{2,1,0:T(8,128)(2,1)S(1)}, u32[]{:S(2)}, u32[]{:S(2)}) collective-permute-start(bf16[8,32,384]{2,1,0:T(8,128)(2,1)S(1)} %get-tuple-element.21), channel_id=1, source_target_pairs={{16,0},{32,16},{48,32},{64,48},{80,64},{96,80},{112,96},{128,112},... | collective-permute-start | bytes 589832 | tf_op jit(solution)/shard_map/ppermute | solution.py:325
  38.4 3.8 %inner.1 = (bf16[1664,384]{1,0:T(8,128)(2,1)S(1)}, bf16[1664,384]{1,0:T(8,128)(2,1)S(1)}, bf16[1920,384]{1,0:T(8,128)(2,1)S(1)}, bf16[512,512]{1,0:T(8,128)(2,1)S(1)}) custom-call(bf16[16,32,384]{2,1,0:T(8,128)(2,1)S(1)} %all-to-all-done.mine_ref, bf16[5,320,320]{2,1,0:T(8,128)(2,1)S(1)} %copy-done.3), custom_call_target="tpu_custom_call" | custom-call | flops 981467136 | bytes 2097152 | tf_op jit(solution)/shard_map/inner/pallas_call | solution.py:206
  42.1 0.0 collective-permute-done.1.refs_0_
  42.1 2.8 %lower.1.refs_5_ = bf16[8,80,128]{2,1,0:T(8,128)(2,1)S(1)} custom-call(bf16[8,32,384]{2,1,0:T(8,128)(2,1)S(1)} %collective-permute-done.1.refs_0_, bf16[1920,384]{1,0:T(8,128)(2,1)S(1)} %get-tuple-element.12.refs_1_, bf16[512,512]{1,0:T(8,128)(2,1)S(1)} %get-tuple-element.13.refs_2_, bf16[1664,384]{1,0:T(8,128)(2,1)S(1)} %get-tuple-element.14.refs_3_, ...), custom_call_target="tpu_custom_call" | custom-call | flops 1308622848 | bytes 2097152 | tf_op jit(solution)/shard_map/lower/pallas_call | solution.py:257
  45.0 0.0 copy-start.1
  45.0 0.0 collective-permute-done.refs_0_
  45.0 3.4 %upper.1 = bf16[16,80,128]{2,1,0:T(8,128)(2,1)} custom-call(bf16[8,32,384]{2,1,0:T(8,128)(2,1)S(1)} %collective-permute-done.refs_0_, bf16[1920,384]{1,0:T(8,128)(2,1)S(1)} %get-tuple-element.12.refs_1_, bf16[512,512]{1,0:T(8,128)(2,1)S(1)} %get-tuple-element.13.refs_2_, bf16[1664,384]{1,0:T(8,128)(2,1)S(1)} %get-tuple-element.14.refs_3_, ...), custom_call_target="tpu_custom_call" | custom-call | flops 1308622848 | bytes 2097152 | tf_op jit(solution)/shard_map/upper/pallas_call | solution.py:257
  48.4 3.5 %all-to-all-start.1 = ((bf16[16,80,128]{2,1,0:T(8,128)(2,1)}), bf16[16,80,128]{2,1,0:T(8,128)(2,1)S(1)}, u32[]{:S(2)}, u32[]{:S(2)}) async-start(bf16[16,80,128]{2,1,0:T(8,128)(2,1)} %upper.1), calls=%async_computation.1 | async-start | bytes 655360 | tf_op jit(solution)/shard_map/all_to_all | solution.py:333
  52.0 12.7 %all-to-all-done.1.back_ref = bf16[16,80,128]{2,1,0:T(8,128)(2,1)S(1)} async-done(((bf16[16,80,128]{2,1,0:T(8,128)(2,1)}), bf16[16,80,128]{2,1,0:T(8,128)(2,1)S(1)}, u32[]{:S(2)}, u32[]{:S(2)}) %all-to-all-start.1) | async-done | bytes 327712 | tf_op jit(solution)/shard_map/all_to_all | solution.py:333
  64.7 0.0 copy-done.1
  64.7 0.3 project.1
  65.1 3.2 %collective-permute-start.2 = (f32[4,16]{1,0:T(4,128)S(1)}, f32[4,16]{1,0:T(4,128)S(1)}, u32[]{:S(2)}, u32[]{:S(2)}) collective-permute-start(f32[4,16]{1,0:T(4,128)S(1)} %get-tuple-element.22), channel_id=1, source_target_pairs={{4,8},{8,4},{12,16},{16,12},{20,24},{24,20},{28,32},{32,28},{36,40... | collective-permute-start | bytes 776 | tf_op jit(solution)/shard_map/ppermute | solution.py:340
  68.2 3.0 %collective-permute-start.3 = (f32[4,16]{1,0:T(4,128)S(1)}, f32[4,16]{1,0:T(4,128)S(1)}, u32[]{:S(2)}, u32[]{:S(2)}) collective-permute-start(f32[4,16]{1,0:T(4,128)S(1)} %get-tuple-element.23), channel_id=1, source_target_pairs={{0,4},{4,0},{8,12},{12,8},{16,20},{20,16},{24,28},{28,24},{32,36},... | collective-permute-start | bytes 776 | tf_op jit(solution)/shard_map/ppermute | solution.py:341
  71.2 1.3 %place.1 = bf16[512,320]{1,0:T(8,128)(2,1)} custom-call(bf16[16,80,128]{2,1,0:T(8,128)(2,1)S(1)} %all-to-all-done.1.back_ref), custom_call_target="tpu_custom_call" | custom-call | flops 201326592 | bytes 2097152 | tf_op jit(solution)/shard_map/place/pallas_call | solution.py:305
  72.5 0.7 collective-permute-done.2
  73.2 0.5 collective-permute-done.3
  73.7 0.6 add_bitcast_fusion
  (9 shorter events, 0.1 us)
Async XLA Ops:
  0.6 10.8 %copy-start.4 = (s32[2,16]{1,0:T(2,128)S(1)}, s32[2,16]{1,0:T(2,128)}, u32[]{:S(2)}) copy-start(s32[2,16]{1,0:T(2,128)} %param.9) | copy-start | bytes 388
  0.6 1.0 %copy-start = (bf16[2,16,16,320]{3,2,1,0:T(8,128)(2,1)S(1)}, bf16[2,16,16,320]{3,2,1,0:T(8,128)(2,1)}, u32[]{:S(2)}) copy-start(bf16[2,16,16,320]{3,2,1,0:T(8,128)(2,1)} %param.5) | copy-start | bytes 983044
  1.6 0.7 copy-start.2
  2.3 36.0 %copy-start.3 = (bf16[5,320,320]{2,1,0:T(8,128)(2,1)S(1)}, bf16[5,320,320]{2,1,0:T(8,128)(2,1)}, u32[]{:S(2)}) copy-start(bf16[5,320,320]{2,1,0:T(8,128)(2,1)} %couplings_ref.1) | copy-start | bytes 3072004
  4.2 21.5 %all-to-all-start = ((bf16[16,32,384]{2,1,0:T(8,128)(2,1)}), bf16[16,32,384]{2,1,0:T(8,128)(2,1)S(1)}, u32[]{:S(2)}, u32[]{:S(2)}) async-start(bf16[16,32,384]{2,1,0:T(8,128)(2,1)} %pack.1), calls=%async_computation | async-start | bytes 786432 | tf_op jit(solution)/shard_map/all_to_all | solution.py:322
  25.7 16.4 %collective-permute-start.1 = (bf16[8,32,384]{2,1,0:T(8,128)(2,1)S(1)}, bf16[8,32,384]{2,1,0:T(8,128)(2,1)S(1)}, u32[]{:S(2)}, u32[]{:S(2)}) collective-permute-start(bf16[8,32,384]{2,1,0:T(8,128)(2,1)S(1)} %get-tuple-element.20), channel_id=1, source_target_pairs={{0,16},{16,32},{32,48},{48,64},{64,80},{80,96},{96,112},{112,128},... | collective-permute-start | bytes 589832 | tf_op jit(solution)/shard_map/ppermute | solution.py:324
  29.1 15.8 %collective-permute-start = (bf16[8,32,384]{2,1,0:T(8,128)(2,1)S(1)}, bf16[8,32,384]{2,1,0:T(8,128)(2,1)S(1)}, u32[]{:S(2)}, u32[]{:S(2)}) collective-permute-start(bf16[8,32,384]{2,1,0:T(8,128)(2,1)S(1)} %get-tuple-element.21), channel_id=1, source_target_pairs={{16,0},{32,16},{48,32},{64,48},{80,64},{96,80},{112,96},{128,112},... | collective-permute-start | bytes 589832 | tf_op jit(solution)/shard_map/ppermute | solution.py:325
  45.0 19.7 %copy-start.1 = (bf16[2,16,320]{2,1,0:T(8,128)(2,1)S(1)}, bf16[2,16,320]{2,1,0:T(8,128)(2,1)}, u32[]{:S(2)}) copy-start(bf16[2,16,320]{2,1,0:T(8,128)(2,1)} %param.8) | copy-start | bytes 61444
  48.4 16.3 %all-to-all-start.1 = ((bf16[16,80,128]{2,1,0:T(8,128)(2,1)}), bf16[16,80,128]{2,1,0:T(8,128)(2,1)S(1)}, u32[]{:S(2)}, u32[]{:S(2)}) async-start(bf16[16,80,128]{2,1,0:T(8,128)(2,1)} %upper.1), calls=%async_computation.1 | async-start | bytes 655360 | tf_op jit(solution)/shard_map/all_to_all | solution.py:333
  65.1 8.2 %collective-permute-start.2 = (f32[4,16]{1,0:T(4,128)S(1)}, f32[4,16]{1,0:T(4,128)S(1)}, u32[]{:S(2)}, u32[]{:S(2)}) collective-permute-start(f32[4,16]{1,0:T(4,128)S(1)} %get-tuple-element.22), channel_id=1, source_target_pairs={{4,8},{8,4},{12,16},{16,12},{20,24},{24,20},{28,32},{32,28},{36,40... | collective-permute-start | bytes 776 | tf_op jit(solution)/shard_map/ppermute | solution.py:340
  68.2 5.5 %collective-permute-start.3 = (f32[4,16]{1,0:T(4,128)S(1)}, f32[4,16]{1,0:T(4,128)S(1)}, u32[]{:S(2)}, u32[]{:S(2)}) collective-permute-start(f32[4,16]{1,0:T(4,128)S(1)} %get-tuple-element.23), channel_id=1, source_target_pairs={{0,4},{4,0},{8,12},{12,8},{16,20},{20,16},{24,28},{28,24},{32,36},... | collective-permute-start | bytes 776 | tf_op jit(solution)/shard_map/ppermute | solution.py:341

commit v5 on v4

--- a/solution.py
+++ b/solution.py
@@ -264,7 +264,15 @@
     )(*args)
 
 
-def project_kernel(back_ref, shapes_ref, column_ref, prev_ref, own_ref, next_ref):
+def project_kernel(back_ref, shapes_ref, map_ref, far_ref, near_ref, own_ref):
+    y = lax.axis_index("y")
+    group = (lax.axis_index("h") * RING + y) * NRAD + lax.axis_index("r")
+    actuator = map_ref[...]
+    column = (((((actuator >> 2) - group) >> 2) + 1) * 4 + (actuator & 3)).astype(F32)
+    same = iota((RADB, RADB), 0) == iota((RADB, RADB), 1)
+    column = jnp.concatenate(
+        [jnp.sum(jnp.where(same, column[a : a + 1, :], 0.0), axis=1, keepdims=True) for a in range(AXB)], axis=0
+    )
     shapes = shapes_ref[...].astype(F32)
     tails = jnp.concatenate([shapes[:RADB, MAIN:], shapes[RADB:, MAIN:]], axis=1)
     back = back_ref[...].astype(F32)
@@ -277,16 +285,21 @@
     by_block = jnp.zeros((BLOCKS, 128), F32)
     for f in range(FORC):
         by_block = jnp.where(lane == f, proj[f], by_block)
-    column = column_ref[...]
-    for at, ref in enumerate((prev_ref, own_ref, next_ref)):
-        for slot in range(4):
-            part = jnp.sum(jnp.where(column == 4 * at + slot, by_block, 0.0), axis=0, keepdims=True)
-            ref[slot : slot + 1, :] = part[:, :FORC]
-
-
-def project(back, shapes, column):
+    parts = [
+        [jnp.sum(jnp.where(column == 4 * at + slot, by_block, 0.0), axis=0, keepdims=True)[:, :FORC] for slot in range(4)]
+        for at in range(3)
+    ]
+    odd = jnp.broadcast_to(y % 2, (1, FORC)) == 1
+    for slot in range(4):
+        to_prev, own, to_next = [part[slot] for part in parts]
+        far_ref[slot : slot + 1, :] = jnp.where(odd, to_next, to_prev)
+        near_ref[slot : slot + 1, :] = jnp.where(odd, to_prev, to_next)
+        own_ref[slot : slot + 1, :] = own
+
+
+def project(back, shapes, amap):
     part = jax.ShapeDtypeStruct((4, FORC), F32)
-    return call(project_kernel, (part, part, part), [], "project", 16, 2 * ROWS * DOF)(back, shapes, column)
+    return call(project_kernel, (part, part, part), [], "project", 16, 2 * ROWS * DOF)(back, shapes, amap)
 
 
 def place_kernel(back_ref, state_ref, wide):
@@ -313,8 +326,6 @@
 
 def body(state, bits, couplings, shapes, amap):
     n_h, n_rad = lax.axis_size("h"), lax.axis_size("r")
-    h, y, r = lax.axis_index("h"), lax.axis_index("y"), lax.axis_index("r")
-    per_group = ACT // (n_h * RING * n_rad)
     ahead = [(i, i + 1) for i in range(n_h - 1)]
     back = [(b, a) for a, b in ahead]
 
@@ -323,22 +334,15 @@
     reach = HALO // AXB * n_rad
     low = lax.ppermute(mine[-reach:], "h", ahead)
     high = lax.ppermute(mine[:reach], "h", back)
-    amap = amap.reshape(BLOCKS, 1)
-    shift = (amap // per_group - ((h * RING + y) * n_rad + r)) // n_rad
-    column = (shift + 1) * per_group + amap % per_group
-    mine, column = lax.optimization_barrier((mine, column))
     fore, adj, keep, masks = inner(mine, couplings)
     lower = outer(False, low, keep, masks, fore, adj)
     out = outer(True, high, keep, masks, fore, adj, lower)
     back_home = lax.all_to_all(out, ("y", "r"), 0, 0, tiled=True)
 
-    to_prev, own, to_next = project(back_home, shapes.reshape(BLOCKS, DOF), column)
+    for_far, for_near, own = project(back_home, shapes.reshape(BLOCKS, DOF), amap)
     n_ax = n_h * RING
-    far = swaps(range(1, n_ax - 1, 2))
-    near = swaps(range(0, n_ax - 1, 2))
-    odd = y % 2 == 1
-    from_far = lax.ppermute(jnp.where(odd, to_next, to_prev), ("h", "y"), far)
-    from_near = lax.ppermute(jnp.where(odd, to_prev, to_next), ("h", "y"), near)
+    from_far = lax.ppermute(for_far, ("h", "y"), swaps(range(1, n_ax - 1, 2)))
+    from_near = lax.ppermute(for_near, ("h", "y"), swaps(range(0, n_ax - 1, 2)))
     result = place(back_home)
     return result.reshape(state.shape), (own + from_far + from_near).T
 

time: 74.7 us -> 72 us (0.964)
  the two profiles are of different devices: /device:TPU:2 before, /device:TPU:768 now
where the time goes in v5:
time: 72 us; the launch traced here: 71.6 us
  blocking collectives  37.2 us (52%)
  starting transfers between devices  16.7 us (23%)
  Pallas kernels  12 us (17%)
  waiting for transfers between devices  2.7 us (4%)
  local copies, waits for them, and re-layouts  1.73 us (2%)
  between operations  0.75 us (1%)
    all_to_all x1, blocking collectives, body(): mine = lax.all_to_all(send, ('y', 'r'), 0, 0, tiled=True)  21.2 us
    all_to_all x1, blocking collectives, body(): back_home = lax.all_to_all(out, ('y', 'r'), 0, 0, tiled=True)  16 us
    ppermute x1, starting transfers between devices, body(): high = lax.ppermute(mine[:reach], 'h', back)  5.77 us
    ppermute x1, starting transfers between devices, body(): from_far = lax.ppermute(for_far, ('h', 'y'), swaps(range(1, n_ax - 1, 2)))  5.59 us
    pallas_call x2, Pallas kernels, outer(): call(functools.partial(outer_kernel, upper), jax.ShapeDtypeStruct((FORC i...  5.54 us
    pallas_call x1, Pallas kernels, inner(): call(inner_kernel, (weights, weights, jax.ShapeDtypeStruct((len(KEEP) * L...  3.77 us
    ppermute x1, starting transfers between devices, body(): low = lax.ppermute(mine[-reach:], 'h', ahead)  3.4 us
    ppermute x1, waiting for transfers between devices, body(): from_far = lax.ppermute(for_far, ('h', 'y'), swaps(range(1, n_ax - 1, 2)))  2.69 us
  transfers between devices with their start and end apart: 4, of which 1 were waited for; matrix products, arithmetic and copies ran while one was open for 0% of the time, Pallas kernels for 11%

profile of v5, /device:TPU:768, one launch (start us, length us, event | category | flops | bytes accessed | tf_op | source)
XLA Modules:
  0.0 71.6 jit_solution(12947488071496275976)
XLA Ops:
  0.6 0.0 copy-start
  0.6 1.0 %copy-done = bf16[2,16,16,320]{3,2,1,0:T(8,128)(2,1)S(1)} copy-done((bf16[2,16,16,320]{3,2,1,0:T(8,128)(2,1)S(1)}, bf16[2,16,16,320]{3,2,1,0:T(8,128)(2,1)}, u32[]{:S(2)}) %copy-start) | copy-done | bytes 327704
  1.6 0.7 copy-done.2
  2.3 1.1 %pack.1 = bf16[16,32,384]{2,1,0:T(8,128)(2,1)S(1)} custom-call(bf16[512,320]{1,0:T(8,128)(2,1)S(1)} %bitcast.6, s32[2,4,16]{2,1,0:T(4,128)S(1)} %bitcast.8), custom_call_target="tpu_custom_call" | custom-call | flops 201326592 | bytes 2097152 | tf_op jit(solution)/shard_map/pack/pallas_call | solution.py:80
  3.4 21.2 %all_to_all.10.mine_ref = bf16[16,32,384]{2,1,0:T(8,128)(2,1)S(1)} all-to-all(bf16[16,32,384]{2,1,0:T(8,128)(2,1)S(1)} %pack.1), channel_id=1, replica_groups=mesh['h'=64,'y'=4,'r'=4] {'y','r'}, dimensions={0} | all-to-all | bytes 786432 | tf_op jit(solution)/shard_map/all_to_all | solution.py:333
  24.7 3.4 %collective-permute-start.1 = (bf16[8,32,384]{2,1,0:T(8,128)(2,1)S(1)}, bf16[8,32,384]{2,1,0:T(8,128)(2,1)S(1)}, u32[]{:S(2)}, u32[]{:S(2)}) collective-permute-start(bf16[8,32,384]{2,1,0:T(8,128)(2,1)S(1)} %get-tuple-element.16), channel_id=1, source_target_pairs={{0,16},{16,32},{32,48},{48,64},{64,80},{80,96},{96,112},{112,128},... | collective-permute-start | bytes 589832 | tf_op jit(solution)/shard_map/ppermute | solution.py:335
  28.1 5.8 %collective-permute-start = (bf16[8,32,384]{2,1,0:T(8,128)(2,1)S(1)}, bf16[8,32,384]{2,1,0:T(8,128)(2,1)S(1)}, u32[]{:S(2)}, u32[]{:S(2)}) collective-permute-start(bf16[8,32,384]{2,1,0:T(8,128)(2,1)S(1)} %get-tuple-element.17), channel_id=1, source_target_pairs={{16,0},{32,16},{48,32},{64,48},{80,64},{96,80},{112,96},{128,112},... | collective-permute-start | bytes 589832 | tf_op jit(solution)/shard_map/ppermute | solution.py:336
  33.9 0.0 copy-done.4
  33.9 3.8 %inner.1 = (bf16[1664,384]{1,0:T(8,128)(2,1)S(1)}, bf16[1664,384]{1,0:T(8,128)(2,1)S(1)}, bf16[1920,384]{1,0:T(8,128)(2,1)S(1)}, bf16[512,512]{1,0:T(8,128)(2,1)S(1)}) custom-call(bf16[16,32,384]{2,1,0:T(8,128)(2,1)S(1)} %all_to_all.10.mine_ref, bf16[5,320,320]{2,1,0:T(8,128)(2,1)S(1)} %copy-done.4), custom_call_target="tpu_custom_call" | custom-call | flops 981467136 | bytes 2097152 | tf_op jit(solution)/shard_map/inner/pallas_call | solution.py:206
  37.7 0.0 collective-permute-done.1.refs_0_
  37.7 2.9 %lower.1.refs_5_ = bf16[8,80,128]{2,1,0:T(8,128)(2,1)S(1)} custom-call(bf16[8,32,384]{2,1,0:T(8,128)(2,1)S(1)} %collective-permute-done.1.refs_0_, bf16[1920,384]{1,0:T(8,128)(2,1)S(1)} %get-tuple-element.9.refs_1_, bf16[512,512]{1,0:T(8,128)(2,1)S(1)} %get-tuple-element.10.refs_2_, bf16[1664,384]{1,0:T(8,128)(2,1)S(1)} %get-tuple-element.11.refs_3_, ...), custom_call_target="tpu_custom_call" | custom-call | flops 1308622848 | bytes 2097152 | tf_op jit(solution)/shard_map/lower/pallas_call | solution.py:257
  40.5 0.0 copy-start.1
  40.6 0.0 copy-start.3
  40.6 0.0 collective-permute-done.refs_0_
  40.6 2.7 %upper.1 = bf16[16,80,128]{2,1,0:T(8,128)(2,1)S(1)} custom-call(bf16[8,32,384]{2,1,0:T(8,128)(2,1)S(1)} %collective-permute-done.refs_0_, bf16[1920,384]{1,0:T(8,128)(2,1)S(1)} %get-tuple-element.9.refs_1_, bf16[512,512]{1,0:T(8,128)(2,1)S(1)} %get-tuple-element.10.refs_2_, bf16[1664,384]{1,0:T(8,128)(2,1)S(1)} %get-tuple-element.11.refs_3_, ...), custom_call_target="tpu_custom_call" | custom-call | flops 1308622848 | bytes 2097152 | tf_op jit(solution)/shard_map/upper/pallas_call | solution.py:257
  43.3 16.0 %all_to_all.11.back_ref = bf16[16,80,128]{2,1,0:T(8,128)(2,1)S(1)} all-to-all(bf16[16,80,128]{2,1,0:T(8,128)(2,1)S(1)} %upper.1), channel_id=1, replica_groups=mesh['h'=64,'y'=4,'r'=4] {'y','r'}, dimensions={0} | all-to-all | bytes 655360 | tf_op jit(solution)/shard_map/all_to_all | solution.py:340
  59.3 0.0 copy-done.3
  59.3 0.3 project.1
  59.6 5.6 %collective-permute-start.2 = (f32[4,16]{1,0:T(4,128)S(1)}, f32[4,16]{1,0:T(4,128)S(1)}, u32[]{:S(2)}, u32[]{:S(2)}) collective-permute-start(f32[4,16]{1,0:T(4,128)S(1)} %get-tuple-element.14), channel_id=1, source_target_pairs={{4,8},{8,4},{12,16},{16,12},{20,24},{24,20},{28,32},{32,28},{36,40... | collective-permute-start | bytes 776 | tf_op jit(solution)/shard_map/ppermute | solution.py:344
  65.2 1.9 %collective-permute-start.3 = (f32[4,16]{1,0:T(4,128)S(1)}, f32[4,16]{1,0:T(4,128)S(1)}, u32[]{:S(2)}, u32[]{:S(2)}) collective-permute-start(f32[4,16]{1,0:T(4,128)S(1)} %get-tuple-element.15), channel_id=1, source_target_pairs={{0,4},{4,0},{8,12},{12,8},{16,20},{20,16},{24,28},{28,24},{32,36},... | collective-permute-start | bytes 776 | tf_op jit(solution)/shard_map/ppermute | solution.py:345
  67.1 1.3 %place.1 = bf16[512,320]{1,0:T(8,128)(2,1)} custom-call(bf16[16,80,128]{2,1,0:T(8,128)(2,1)S(1)} %all_to_all.11.back_ref), custom_call_target="tpu_custom_call" | custom-call | flops 201326592 | bytes 2097152 | tf_op jit(solution)/shard_map/place/pallas_call | solution.py:318
  68.4 2.7 %collective-permute-done.2 = f32[4,16]{1,0:T(4,128)S(1)} collective-permute-done((f32[4,16]{1,0:T(4,128)S(1)}, f32[4,16]{1,0:T(4,128)S(1)}, u32[]{:S(2)}, u32[]{:S(2)}) %collective-permute-start.2) | collective-permute-done | bytes 288 | tf_op jit(solution)/shard_map/ppermute | solution.py:344
  71.1 0.0 collective-permute-done.3
  71.1 0.6 add_bitcast_fusion
  (4 shorter events, 0.0 us)
Async XLA Ops:
  0.6 1.0 %copy-start = (bf16[2,16,16,320]{3,2,1,0:T(8,128)(2,1)S(1)}, bf16[2,16,16,320]{3,2,1,0:T(8,128)(2,1)}, u32[]{:S(2)}) copy-start(bf16[2,16,16,320]{3,2,1,0:T(8,128)(2,1)} %param.5) | copy-start | bytes 983044
  1.6 0.7 copy-start.2
  2.3 31.6 %copy-start.4 = (bf16[5,320,320]{2,1,0:T(8,128)(2,1)S(1)}, bf16[5,320,320]{2,1,0:T(8,128)(2,1)}, u32[]{:S(2)}) copy-start(bf16[5,320,320]{2,1,0:T(8,128)(2,1)} %couplings_ref.1) | copy-start | bytes 3072004
  24.7 13.0 %collective-permute-start.1 = (bf16[8,32,384]{2,1,0:T(8,128)(2,1)S(1)}, bf16[8,32,384]{2,1,0:T(8,128)(2,1)S(1)}, u32[]{:S(2)}, u32[]{:S(2)}) collective-permute-start(bf16[8,32,384]{2,1,0:T(8,128)(2,1)S(1)} %get-tuple-element.16), channel_id=1, source_target_pairs={{0,16},{16,32},{32,48},{48,64},{64,80},{80,96},{96,112},{112,128},... | collective-permute-start | bytes 589832 | tf_op jit(solution)/shard_map/ppermute | solution.py:335
  28.1 12.4 %collective-permute-start = (bf16[8,32,384]{2,1,0:T(8,128)(2,1)S(1)}, bf16[8,32,384]{2,1,0:T(8,128)(2,1)S(1)}, u32[]{:S(2)}, u32[]{:S(2)}) collective-permute-start(bf16[8,32,384]{2,1,0:T(8,128)(2,1)S(1)} %get-tuple-element.17), channel_id=1, source_target_pairs={{16,0},{32,16},{48,32},{64,48},{80,64},{96,80},{112,96},{128,112},... | collective-permute-start | bytes 589832 | tf_op jit(solution)/shard_map/ppermute | solution.py:336
  40.5 18.7 %copy-start.1 = (bf16[2,16,320]{2,1,0:T(8,128)(2,1)S(1)}, bf16[2,16,320]{2,1,0:T(8,128)(2,1)}, u32[]{:S(2)}) copy-start(bf16[2,16,320]{2,1,0:T(8,128)(2,1)} %param.8) | copy-start | bytes 61444
  40.6 18.7 %copy-start.3 = (s32[2,16]{1,0:T(2,128)S(1)}, s32[2,16]{1,0:T(2,128)}, u32[]{:S(2)}) copy-start(s32[2,16]{1,0:T(2,128)} %map_ref.1) | copy-start | bytes 388
  59.6 11.5 %collective-permute-start.2 = (f32[4,16]{1,0:T(4,128)S(1)}, f32[4,16]{1,0:T(4,128)S(1)}, u32[]{:S(2)}, u32[]{:S(2)}) collective-permute-start(f32[4,16]{1,0:T(4,128)S(1)} %get-tuple-element.14), channel_id=1, source_target_pairs={{4,8},{8,4},{12,16},{16,12},{20,24},{24,20},{28,32},{32,28},{36,40... | collective-permute-start | bytes 776 | tf_op jit(solution)/shard_map/ppermute | solution.py:344
  65.2 5.9 %collective-permute-start.3 = (f32[4,16]{1,0:T(4,128)S(1)}, f32[4,16]{1,0:T(4,128)S(1)}, u32[]{:S(2)}, u32[]{:S(2)}) collective-permute-start(f32[4,16]{1,0:T(4,128)S(1)} %get-tuple-element.15), channel_id=1, source_target_pairs={{0,4},{4,0},{8,12},{12,8},{16,20},{20,16},{24,28},{28,24},{32,36},... | collective-permute-start | bytes 776 | tf_op jit(solution)/shard_map/ppermute | solution.py:345

commit v6 on v5

--- a/solution.py
+++ b/solution.py
@@ -108,7 +108,12 @@
         ref[5 * MAIN + at * 64 : 5 * MAIN + (at + 1) * 64, :] = value[MAIN:].astype(BF)
 
     for at in range(5):
-        put(fore_ref, at, dot(couplings_ref[at], twice))
+        matrix = couplings_ref[at]
+        tail = dot(matrix, twice[:, MAIN:]).astype(BF)
+        fore_ref[at * MAIN : (at + 1) * MAIN, :MAIN] = matrix[:MAIN, :MAIN]
+        fore_ref[at * MAIN : (at + 1) * MAIN, MAIN:] = tail[:MAIN]
+        fore_ref[5 * MAIN + at * 64 : 5 * MAIN + (at + 1) * 64, :MAIN] = matrix[MAIN:, :MAIN]
+        fore_ref[5 * MAIN + at * 64 : 5 * MAIN + (at + 1) * 64, MAIN:] = tail[MAIN:]
     for at, e in enumerate((0, 2, 1, 4, 3)):
         matrix = couplings_ref[e]
         put(adj_ref, at, dot_nt(same, jnp.concatenate([matrix, matrix[MAIN:]], axis=0)))

time: 72 us -> 71.7 us (level)
  no operation moved by 1% of the time
where the time goes in v6:
time: 71.7 us; the launch traced here: 71.4 us
  blocking collectives  37.2 us (52%)
  starting transfers between devices  16.9 us (24%)
  Pallas kernels  11.7 us (16%)
  waiting for transfers between devices  2.44 us (3%)
  local copies, waits for them, and re-layouts  1.73 us (2%)
  between operations  0.75 us (1%)
    all_to_all x1, blocking collectives, body(): mine = lax.all_to_all(send, ('y', 'r'), 0, 0, tiled=True)  21.2 us
    all_to_all x1, blocking collectives, body(): back_home = lax.all_to_all(out, ('y', 'r'), 0, 0, tiled=True)  16 us
    ppermute x1, starting transfers between devices, body(): from_far = lax.ppermute(for_far, ('h', 'y'), swaps(range(1, n_ax - 1, 2)))  5.85 us
    ppermute x1, starting transfers between devices, body(): high = lax.ppermute(mine[:reach], 'h', back)  5.77 us
    pallas_call x2, Pallas kernels, outer(): call(functools.partial(outer_kernel, upper), jax.ShapeDtypeStruct((FORC i...  5.53 us
    pallas_call x1, Pallas kernels, inner(): call(inner_kernel, (weights, weights, jax.ShapeDtypeStruct((len(KEEP) * L...  3.52 us
    ppermute x1, starting transfers between devices, body(): low = lax.ppermute(mine[-reach:], 'h', ahead)  3.4 us
    ppermute x1, waiting for transfers between devices, body(): from_far = lax.ppermute(for_far, ('h', 'y'), swaps(range(1, n_ax - 1, 2)))  2.43 us
  transfers between devices with their start and end apart: 4, of which 1 were waited for; matrix products, arithmetic and copies ran while one was open for 0% of the time, Pallas kernels for 11%

profile of v6, /device:TPU:768, one launch (start us, length us, event | category | flops | bytes accessed | tf_op | source)
XLA Modules:
  0.0 71.4 jit_solution(658668421484527424)
XLA Ops:
  0.6 0.0 copy-start
  0.6 1.0 %copy-done = bf16[2,16,16,320]{3,2,1,0:T(8,128)(2,1)S(1)} copy-done((bf16[2,16,16,320]{3,2,1,0:T(8,128)(2,1)S(1)}, bf16[2,16,16,320]{3,2,1,0:T(8,128)(2,1)}, u32[]{:S(2)}) %copy-start) | copy-done | bytes 327704
  1.6 0.7 copy-done.2
  2.3 1.1 %pack.1 = bf16[16,32,384]{2,1,0:T(8,128)(2,1)S(1)} custom-call(bf16[512,320]{1,0:T(8,128)(2,1)S(1)} %bitcast.6, s32[2,4,16]{2,1,0:T(4,128)S(1)} %bitcast.8), custom_call_target="tpu_custom_call" | custom-call | flops 201326592 | bytes 2097152 | tf_op jit(solution)/shard_map/pack/pallas_call | solution.py:80
  3.4 21.2 %all_to_all.10.mine_ref = bf16[16,32,384]{2,1,0:T(8,128)(2,1)S(1)} all-to-all(bf16[16,32,384]{2,1,0:T(8,128)(2,1)S(1)} %pack.1), channel_id=1, replica_groups=mesh['h'=64,'y'=4,'r'=4] {'y','r'}, dimensions={0} | all-to-all | bytes 786432 | tf_op jit(solution)/shard_map/all_to_all | solution.py:338
  24.7 3.4 %collective-permute-start.1 = (bf16[8,32,384]{2,1,0:T(8,128)(2,1)S(1)}, bf16[8,32,384]{2,1,0:T(8,128)(2,1)S(1)}, u32[]{:S(2)}, u32[]{:S(2)}) collective-permute-start(bf16[8,32,384]{2,1,0:T(8,128)(2,1)S(1)} %get-tuple-element.16), channel_id=1, source_target_pairs={{0,16},{16,32},{32,48},{48,64},{64,80},{80,96},{96,112},{112,128},... | collective-permute-start | bytes 589832 | tf_op jit(solution)/shard_map/ppermute | solution.py:340
  28.1 5.8 %collective-permute-start = (bf16[8,32,384]{2,1,0:T(8,128)(2,1)S(1)}, bf16[8,32,384]{2,1,0:T(8,128)(2,1)S(1)}, u32[]{:S(2)}, u32[]{:S(2)}) collective-permute-start(bf16[8,32,384]{2,1,0:T(8,128)(2,1)S(1)} %get-tuple-element.17), channel_id=1, source_target_pairs={{16,0},{32,16},{48,32},{64,48},{80,64},{96,80},{112,96},{128,112},... | collective-permute-start | bytes 589832 | tf_op jit(solution)/shard_map/ppermute | solution.py:341
  33.9 0.0 copy-done.4
  33.9 3.5 %inner.1 = (bf16[1664,384]{1,0:T(8,128)(2,1)S(1)}, bf16[1664,384]{1,0:T(8,128)(2,1)S(1)}, bf16[1920,384]{1,0:T(8,128)(2,1)S(1)}, bf16[512,512]{1,0:T(8,128)(2,1)S(1)}) custom-call(bf16[16,32,384]{2,1,0:T(8,128)(2,1)S(1)} %all_to_all.10.mine_ref, bf16[5,320,320]{2,1,0:T(8,128)(2,1)S(1)} %copy-done.4), custom_call_target="tpu_custom_call" | custom-call | flops 981467136 | bytes 2097152 | tf_op jit(solution)/shard_map/inner/pallas_call | solution.py:211
  37.4 0.0 collective-permute-done.1.refs_0_
  37.4 2.8 %lower.1.refs_5_ = bf16[8,80,128]{2,1,0:T(8,128)(2,1)S(1)} custom-call(bf16[8,32,384]{2,1,0:T(8,128)(2,1)S(1)} %collective-permute-done.1.refs_0_, bf16[1920,384]{1,0:T(8,128)(2,1)S(1)} %get-tuple-element.9.refs_1_, bf16[512,512]{1,0:T(8,128)(2,1)S(1)} %get-tuple-element.10.refs_2_, bf16[1664,384]{1,0:T(8,128)(2,1)S(1)} %get-tuple-element.11.refs_3_, ...), custom_call_target="tpu_custom_call" | custom-call | flops 1308622848 | bytes 2097152 | tf_op jit(solution)/shard_map/lower/pallas_call | solution.py:262
  40.3 0.0 copy-start.1
  40.3 0.0 copy-start.3
  40.3 0.0 collective-permute-done.refs_0_
  40.3 2.7 %upper.1 = bf16[16,80,128]{2,1,0:T(8,128)(2,1)S(1)} custom-call(bf16[8,32,384]{2,1,0:T(8,128)(2,1)S(1)} %collective-permute-done.refs_0_, bf16[1920,384]{1,0:T(8,128)(2,1)S(1)} %get-tuple-element.9.refs_1_, bf16[512,512]{1,0:T(8,128)(2,1)S(1)} %get-tuple-element.10.refs_2_, bf16[1664,384]{1,0:T(8,128)(2,1)S(1)} %get-tuple-element.11.refs_3_, ...), custom_call_target="tpu_custom_call" | custom-call | flops 1308622848 | bytes 2097152 | tf_op jit(solution)/shard_map/upper/pallas_call | solution.py:262
  43.0 16.0 %all_to_all.11.back_ref = bf16[16,80,128]{2,1,0:T(8,128)(2,1)S(1)} all-to-all(bf16[16,80,128]{2,1,0:T(8,128)(2,1)S(1)} %upper.1), channel_id=1, replica_groups=mesh['h'=64,'y'=4,'r'=4] {'y','r'}, dimensions={0} | all-to-all | bytes 655360 | tf_op jit(solution)/shard_map/all_to_all | solution.py:345
  59.0 0.0 copy-done.3
  59.0 0.3 project.1
  59.3 5.9 %collective-permute-start.2 = (f32[4,16]{1,0:T(4,128)S(1)}, f32[4,16]{1,0:T(4,128)S(1)}, u32[]{:S(2)}, u32[]{:S(2)}) collective-permute-start(f32[4,16]{1,0:T(4,128)S(1)} %get-tuple-element.14), channel_id=1, source_target_pairs={{4,8},{8,4},{12,16},{16,12},{20,24},{24,20},{28,32},{32,28},{36,40... | collective-permute-start | bytes 776 | tf_op jit(solution)/shard_map/ppermute | solution.py:349
  65.2 1.9 %collective-permute-start.3 = (f32[4,16]{1,0:T(4,128)S(1)}, f32[4,16]{1,0:T(4,128)S(1)}, u32[]{:S(2)}, u32[]{:S(2)}) collective-permute-start(f32[4,16]{1,0:T(4,128)S(1)} %get-tuple-element.15), channel_id=1, source_target_pairs={{0,4},{4,0},{8,12},{12,8},{16,20},{20,16},{24,28},{28,24},{32,36},... | collective-permute-start | bytes 776 | tf_op jit(solution)/shard_map/ppermute | solution.py:350
  67.1 1.3 %place.1 = bf16[512,320]{1,0:T(8,128)(2,1)} custom-call(bf16[16,80,128]{2,1,0:T(8,128)(2,1)S(1)} %all_to_all.11.back_ref), custom_call_target="tpu_custom_call" | custom-call | flops 201326592 | bytes 2097152 | tf_op jit(solution)/shard_map/place/pallas_call | solution.py:323
  68.4 2.4 %collective-permute-done.2 = f32[4,16]{1,0:T(4,128)S(1)} collective-permute-done((f32[4,16]{1,0:T(4,128)S(1)}, f32[4,16]{1,0:T(4,128)S(1)}, u32[]{:S(2)}, u32[]{:S(2)}) %collective-permute-start.2) | collective-permute-done | bytes 288 | tf_op jit(solution)/shard_map/ppermute | solution.py:349
  70.8 0.0 collective-permute-done.3
  70.8 0.6 add_bitcast_fusion
  (4 shorter events, 0.0 us)
Async XLA Ops:
  0.6 1.0 %copy-start = (bf16[2,16,16,320]{3,2,1,0:T(8,128)(2,1)S(1)}, bf16[2,16,16,320]{3,2,1,0:T(8,128)(2,1)}, u32[]{:S(2)}) copy-start(bf16[2,16,16,320]{3,2,1,0:T(8,128)(2,1)} %param.5) | copy-start | bytes 983044
  1.6 0.7 copy-start.2
  2.3 31.6 %copy-start.4 = (bf16[5,320,320]{2,1,0:T(8,128)(2,1)S(1)}, bf16[5,320,320]{2,1,0:T(8,128)(2,1)}, u32[]{:S(2)}) copy-start(bf16[5,320,320]{2,1,0:T(8,128)(2,1)} %couplings_ref.1) | copy-start | bytes 3072004
  24.7 12.7 %collective-permute-start.1 = (bf16[8,32,384]{2,1,0:T(8,128)(2,1)S(1)}, bf16[8,32,384]{2,1,0:T(8,128)(2,1)S(1)}, u32[]{:S(2)}, u32[]{:S(2)}) collective-permute-start(bf16[8,32,384]{2,1,0:T(8,128)(2,1)S(1)} %get-tuple-element.16), channel_id=1, source_target_pairs={{0,16},{16,32},{32,48},{48,64},{64,80},{80,96},{96,112},{112,128},... | collective-permute-start | bytes 589832 | tf_op jit(solution)/shard_map/ppermute | solution.py:340
  28.1 12.2 %collective-permute-start = (bf16[8,32,384]{2,1,0:T(8,128)(2,1)S(1)}, bf16[8,32,384]{2,1,0:T(8,128)(2,1)S(1)}, u32[]{:S(2)}, u32[]{:S(2)}) collective-permute-start(bf16[8,32,384]{2,1,0:T(8,128)(2,1)S(1)} %get-tuple-element.17), channel_id=1, source_target_pairs={{16,0},{32,16},{48,32},{64,48},{80,64},{96,80},{112,96},{128,112},... | collective-permute-start | bytes 589832 | tf_op jit(solution)/shard_map/ppermute | solution.py:341
  40.3 18.7 %copy-start.1 = (bf16[2,16,320]{2,1,0:T(8,128)(2,1)S(1)}, bf16[2,16,320]{2,1,0:T(8,128)(2,1)}, u32[]{:S(2)}) copy-start(bf16[2,16,320]{2,1,0:T(8,128)(2,1)} %param.8) | copy-start | bytes 61444
  40.3 18.7 %copy-start.3 = (s32[2,16]{1,0:T(2,128)S(1)}, s32[2,16]{1,0:T(2,128)}, u32[]{:S(2)}) copy-start(s32[2,16]{1,0:T(2,128)} %map_ref.1) | copy-start | bytes 388
  59.3 11.5 %collective-permute-start.2 = (f32[4,16]{1,0:T(4,128)S(1)}, f32[4,16]{1,0:T(4,128)S(1)}, u32[]{:S(2)}, u32[]{:S(2)}) collective-permute-start(f32[4,16]{1,0:T(4,128)S(1)} %get-tuple-element.14), channel_id=1, source_target_pairs={{4,8},{8,4},{12,16},{16,12},{20,24},{24,20},{28,32},{32,28},{36,40... | collective-permute-start | bytes 776 | tf_op jit(solution)/shard_map/ppermute | solution.py:349
  65.2 5.6 %collective-permute-start.3 = (f32[4,16]{1,0:T(4,128)S(1)}, f32[4,16]{1,0:T(4,128)S(1)}, u32[]{:S(2)}, u32[]{:S(2)}) collective-permute-start(f32[4,16]{1,0:T(4,128)S(1)} %get-tuple-element.15), channel_id=1, source_target_pairs={{0,4},{4,0},{8,12},{12,8},{16,20},{20,16},{24,28},{28,24},{32,36},... | collective-permute-start | bytes 776 | tf_op jit(solution)/shard_map/ppermute | solution.py:350
